TPU v7x, 1024 devices: a whole 4x8x16 slice. The times are simulated.
1024 devices in a mesh: gz: 128 (over x, z, core), gy: 8 (over y).
Axes of the slice: x: 4, y: 8, z: 16, core: 2. Of those that a mesh axis runs over, the one named last changes fastest.
Arguments:
- velocity: float32 [3, 2048, 128, 256], P(None, 'gz', 'gy'), may hold values from -14 to 14
Outputs:
- increment: float32 [3, 2048, 128, 256], P(None, 'gz', 'gy')
All inputs are finite; a program needn't handle non-finite values. Where the computation divides by a largest or mean magnitude, that divisor is 1e-20 or more.
Results may differ from a plain program's by a relative error of at most 0.00011.
Values sent between devices are 32-bit elements; how exact they have to be, the bound alone decides.
No kernel may reach another device: no remote copies, remote signals or barrier semaphores. Data moves between devices by JAX's collectives and lax.ppermute only.
A program may use at most 64 MiB of HBM per device.

v0:
```python
import jax
import jax.numpy as jnp
from jax import lax
from jax.sharding import PartitionSpec as P

FIRST_NEAR = 14.0 / 9.0
FIRST_FAR = 1.0 / 9.0
SECOND_NEAR = 12.0 / 11.0
SECOND_FAR = 3.0 / 11.0
VISCOSITY = 1.0
COURANT = 4.0
FIRST_ROOT = -0.38196601125010515
SECOND_ROOT = -0.18826230851010056


def shifted_2(value, axis, steps):
    count = lax.axis_size(axis)
    pairs = [(source, (source + steps) % count) for source in range(count)]
    return lax.ppermute(value, axis, pairs)


def extended(block, sides, width):
    for axis, dim in sides:
        count = lax.axis_size(axis)
        forward = [(i, i + 1) for i in range(count - 1)]
        forward.append((count - 1, 0))
        backward = [(target, source) for source, target in forward]
        low = lax.ppermute(
            lax.slice_in_dim(block, block.shape[dim] - width, None, axis=dim), axis, forward
        )
        high = lax.ppermute(lax.slice_in_dim(block, 0, width, axis=dim), axis, backward)
        block = jnp.concatenate([low, block, high], axis=dim)
    return block


def signed_power(base, exponent):
    magnitude = jnp.exp(exponent.astype(jnp.float32) * jnp.log(jnp.abs(base)))
    return jnp.where(exponent % 2 == 1, -magnitude, magnitude)


def cycle_pass(values, factors, reverse):
    planes = values.shape[1]
    factor_cube = factors[:, None, None]
    rows = lax.broadcasted_iota(jnp.int32, (planes, planes), 0)
    cols = lax.broadcasted_iota(jnp.int32, (planes, planes), 1)
    gaps = cols - rows if reverse else rows - cols
    kernel_table = jnp.where(
        gaps[None] >= 0, signed_power(factor_cube, jnp.maximum(gaps, 0)[None]), 0.0
    )
    plane_ids = jnp.arange(planes, dtype=jnp.int32)
    steps_up = planes - plane_ids if reverse else plane_ids + 1
    lift_rows = signed_power(factors[:, None], steps_up[None])
    end_row = 0 if reverse else planes - 1
    local_part = jnp.einsum("sjm,smyx->sjyx", kernel_table, values, precision=lax.Precision.HIGHEST)
    end_values = local_part[:, end_row]
    if reverse:
        carry_in = shifted_2(end_values, "gz", -1)
    else:
        carry_in = shifted_2(end_values, "gz", 1)
    return local_part + lift_rows[:, :, None, None] * carry_in[:, None]


def body(velocity):
    planes = velocity.shape[1]
    local_highest = jnp.max(jnp.sum(jnp.abs(velocity), axis=0))
    highest = lax.pmax(local_highest, ("gz", "gy"))
    step_size = COURANT / (highest + 1e-06)
    widened = extended(velocity, (("gz", 1),), 2)
    fluxes = widened[2][None] * widened

    def shifted(field, offset):
        return lax.slice_in_dim(field, 2 + offset, 2 + offset + planes, axis=1)

    first_rhs = 0.5 * FIRST_NEAR * (shifted(fluxes, 1) - shifted(fluxes, -1)) + 0.25 * FIRST_FAR * (
        shifted(fluxes, 2) - shifted(fluxes, -2)
    )
    second_rhs = SECOND_NEAR * (
        shifted(widened, 1) - 2.0 * velocity + shifted(widened, -1)
    ) + 0.25 * SECOND_FAR * (shifted(widened, 2) - 2.0 * velocity + shifted(widened, -2))
    sources = jnp.concatenate([first_rhs, second_rhs], axis=0)
    factors = jnp.array([FIRST_ROOT] * 3 + [SECOND_ROOT] * 3, dtype=jnp.float32)
    forward = cycle_pass(sources, factors, False)
    backward = cycle_pass(forward, factors, True)
    solved = (1.0 + factors * factors)[:, None, None, None] * backward
    return step_size * (VISCOSITY * solved[3:] - solved[:3])


def solution(mesh):
    return jax.shard_map(
        body,
        mesh=mesh,
        in_specs=(P(None, "gz", "gy", None),),
        out_specs=P(None, "gz", "gy", None),
        check_vma=False,
    )
```

profile of v0, /device:TPU:1, one launch (start us, length us, event | category | flops | bytes accessed | tf_op | source)
XLA Modules:
  0.0 165.6 jit_solution(9370992537680107743)
XLA Ops:
  0.0 0.0 copy-start.1
  0.0 1.6 constant_dynamic-update-slice_fusion.1
  1.6 0.1 fusion.64
  1.7 5.4 %collective-permute-start = (f32[3,2,16,256]{3,1,2,0:T(2,128)S(1)}, f32[3,2,16,256]{3,1,2,0:T(2,128)S(1)}, u32[]{:S(2)}, u32[]{:S(2)}) collective-permute-start(f32[3,2,16,256]{3,1,2,0:T(2,128)S(1)} %get-tuple-element.6), channel_id=1, source_target_pairs={{0,8},{8,16},{16,24},{24,32},{32,40},{40,48},{48,56},{56,64},{64,7... | collective-permute-start | bytes 294920 | tf_op jit(solution)/shard_map/ppermute | solution.py:28
  7.1 12.6 %collective-permute-start.1 = (f32[3,2,16,256]{3,1,2,0:T(2,128)S(1)}, f32[3,2,16,256]{3,1,2,0:T(2,128)S(1)}, u32[]{:S(2)}, u32[]{:S(2)}) collective-permute-start(f32[3,2,16,256]{3,1,2,0:T(2,128)S(1)} %get-tuple-element.5), channel_id=1, source_target_pairs={{8,0},{16,8},{24,16},{32,24},{40,32},{48,40},{56,48},{64,56},{72,6... | collective-permute-start | bytes 294920 | tf_op jit(solution)/shard_map/ppermute | solution.py:31
  19.7 0.0 copy-done.1
  19.8 0.1 negate_select_fusion.2
  19.9 0.0 collective-permute-done
  19.9 0.7 collective-permute-done.1
  20.6 0.2 pad_maximum_fusion
  20.8 0.2 broadcast_multiply_fusion
  21.1 0.8 fusion.10
  21.9 1.5 fusion
  23.4 0.1 slice.75
  23.5 1.9 %collective-permute-start.2 = (f32[6,16,256]{2,1,0:T(8,128)S(1)}, f32[6,16,256]{2,1,0:T(8,128)S(1)}, u32[]{:S(2)}, u32[]{:S(2)}) collective-permute-start(f32[6,16,256]{2,1,0:T(8,128)S(1)} %bitcast.19), channel_id=1, source_target_pairs={{0,8},{8,16},{16,24},{24,32},{32,40},{40,48},{48,56},{56,64},{64,7... | collective-permute-start | bytes 294920 | tf_op jit(solution)/shard_map/ppermute | solution.py:19
  25.4 7.3 %collective-permute-done.2 = f32[6,16,256]{2,1,0:T(8,128)S(1)} collective-permute-done((f32[6,16,256]{2,1,0:T(8,128)S(1)}, f32[6,16,256]{2,1,0:T(8,128)S(1)}, u32[]{:S(2)}, u32[]{:S(2)}) %collective-permute-start.2) | collective-permute-done | bytes 98336 | tf_op jit(solution)/shard_map/ppermute | solution.py:19
  32.7 0.0 copy-start
  32.7 1.5 fusion.4
  34.3 0.0 copy-start.2
  34.3 0.1 slice.76
  34.4 8.6 %collective-permute-start.3 = (f32[6,16,256]{2,1,0:T(8,128)S(1)}, f32[6,16,256]{2,1,0:T(8,128)S(1)}, u32[]{:S(2)}, u32[]{:S(2)}) collective-permute-start(f32[6,16,256]{2,1,0:T(8,128)S(1)} %bitcast.18), channel_id=1, source_target_pairs={{0,1016},{8,0},{16,8},{24,16},{32,24},{40,32},{48,40},{56,48},{64,... | collective-permute-start | bytes 294920 | tf_op jit(solution)/shard_map/ppermute | solution.py:19
  42.9 0.0 copy-done
  42.9 0.1 abs_reduce_fusion
  43.0 0.7 reduce_max.9
  43.7 119.4 %pmax.7 = f32[]{:T(128)} all-reduce(f32[]{:T(128)} %reduce_max.9), channel_id=1, replica_groups=mesh['gz'=128,'gy'=8] {'gz','gy'}, use_global_device_ids=true, to_apply=%region_2.0 | all-reduce | flops 1 | bytes 8 | tf_op jit(solution)/shard_map/pmax | solution.py:66
  163.8 0.0 collective-permute-done.3
  163.8 0.0 copy-done.2
  163.8 0.3 add_multiply_fusion
  164.1 0.2 fusion.11
  164.3 1.3 copy.16
  (10 shorter events, 0.1 us)
Async XLA Ops:
  0.0 19.7 %copy-start.1 = (f32[6]{0:T(128)S(1)}, f32[6]{0:T(128)}, u32[]{:S(2)}) copy-start(f32[6]{0:T(128)} %constant.69) | copy-start | bytes 76
  1.7 18.2 %collective-permute-start = (f32[3,2,16,256]{3,1,2,0:T(2,128)S(1)}, f32[3,2,16,256]{3,1,2,0:T(2,128)S(1)}, u32[]{:S(2)}, u32[]{:S(2)}) collective-permute-start(f32[3,2,16,256]{3,1,2,0:T(2,128)S(1)} %get-tuple-element.6), channel_id=1, source_target_pairs={{0,8},{8,16},{16,24},{24,32},{32,40},{40,48},{48,56},{56,64},{64,7... | collective-permute-start | bytes 294920 | tf_op jit(solution)/shard_map/ppermute | solution.py:28
  7.1 13.5 %collective-permute-start.1 = (f32[3,2,16,256]{3,1,2,0:T(2,128)S(1)}, f32[3,2,16,256]{3,1,2,0:T(2,128)S(1)}, u32[]{:S(2)}, u32[]{:S(2)}) collective-permute-start(f32[3,2,16,256]{3,1,2,0:T(2,128)S(1)} %get-tuple-element.5), channel_id=1, source_target_pairs={{8,0},{16,8},{24,16},{32,24},{40,32},{48,40},{56,48},{64,56},{72,6... | collective-permute-start | bytes 294920 | tf_op jit(solution)/shard_map/ppermute | solution.py:31
  23.5 9.3 %collective-permute-start.2 = (f32[6,16,256]{2,1,0:T(8,128)S(1)}, f32[6,16,256]{2,1,0:T(8,128)S(1)}, u32[]{:S(2)}, u32[]{:S(2)}) collective-permute-start(f32[6,16,256]{2,1,0:T(8,128)S(1)} %bitcast.19), channel_id=1, source_target_pairs={{0,8},{8,16},{16,24},{24,32},{32,40},{40,48},{48,56},{56,64},{64,7... | collective-permute-start | bytes 294920 | tf_op jit(solution)/shard_map/ppermute | solution.py:19
  32.7 10.2 %copy-start = (f32[3,16,16,256]{3,2,1,0:T(8,128)S(1)}, f32[3,16,16,256]{3,2,1,0:T(8,128)}, u32[]{:S(2)}) copy-start(f32[3,16,16,256]{3,2,1,0:T(8,128)} %param.2) | copy-start | bytes 2359300
  34.3 129.5 %copy-start.2 = (f32[6]{0:T(128)S(1)}, f32[6]{0:T(128)}, u32[]{:S(2)}) copy-start(f32[6]{0:T(128)} %constant.67) | copy-start | bytes 76
  34.4 129.4 %collective-permute-start.3 = (f32[6,16,256]{2,1,0:T(8,128)S(1)}, f32[6,16,256]{2,1,0:T(8,128)S(1)}, u32[]{:S(2)}, u32[]{:S(2)}) collective-permute-start(f32[6,16,256]{2,1,0:T(8,128)S(1)} %bitcast.18), channel_id=1, source_target_pairs={{0,1016},{8,0},{16,8},{24,16},{32,24},{40,32},{48,40},{56,48},{64,... | collective-permute-start | bytes 294920 | tf_op jit(solution)/shard_map/ppermute | solution.py:19
where the time goes:
time: 166 us
  blocking collectives  119 us (72%)
  starting transfers between devices  28.5 us (17%)
  waiting for transfers between devices  8.07 us (5%)
  local copies, waits for them, and re-layouts  3.29 us (2%)
  matrix products  2.99 us (2%)
  other arithmetic  2.51 us (2%)
    pmax x1, blocking collectives, body(): highest = lax.pmax(local_highest, ('gz', 'gy'))  119 us
    ppermute x1, starting transfers between devices, extended(): lax.ppermute(lax.slice_in_dim(block, 0, width, axis=dim), axis, backward)  12.6 us
    ppermute x2, starting transfers between devices, shifted_2(): return lax.ppermute(value, axis, pairs)  10.5 us
    ppermute x2, waiting for transfers between devices, shifted_2(): return lax.ppermute(value, axis, pairs)  7.32 us
    ppermute x1, starting transfers between devices, extended(): lax.ppermute(lax.slice_in_dim(block, block.shape[dim] - width, None, axis...  5.39 us
  transfers between devices with their start and end apart: 4, of which 2 were waited for; matrix products, arithmetic and copies ran while one was open for 1% of the time, Pallas kernels for 0%

commit v1 on v0

v1 whole, which is shorter than its diff:
```python
import jax
import jax.numpy as jnp
from jax import lax
from jax.experimental import pallas as pl
from jax.experimental.pallas import tpu as pltpu
from jax.sharding import PartitionSpec as P

COURANT = 4.0
FIRST_ROOT = -0.38196601125010515
SECOND_ROOT = -0.18826230851010056
FIRST_OFF, FIRST_NEAR, FIRST_FAR = 1.0 / 3.0, 7.0 / 9.0, 1.0 / 36.0
SECOND_OFF, SECOND_NEAR, SECOND_FAR = 2.0 / 11.0, 12.0 / 11.0, 3.0 / 44.0


def filter_constants():
    r = FIRST_ROOT
    gain = 1.0 / (1.0 + 2.0 * FIRST_OFF * r)
    tail = gain * (FIRST_NEAR * (r - 1.0 / r) + FIRST_FAR * (r * r - 1.0 / (r * r)))
    first = (r, -tail * r / (1.0 - r), -gain * FIRST_FAR * (r - 1.0 / r))
    r = SECOND_ROOT
    gain = 1.0 / (1.0 + 2.0 * SECOND_OFF * r)
    tail = gain * (
        SECOND_NEAR * (r + 1.0 / r)
        + SECOND_FAR * (r * r + 1.0 / (r * r))
        - 2.0 * (SECOND_NEAR + SECOND_FAR)
    )
    second = (r, -tail * r / (1.0 - r), gain * SECOND_FAR * (r - 1.0 / r))
    return first, second


(R1, A1, E1), (R2, A2, E2) = filter_constants()


def edges_kernel(vel, peak, rightward, leftward):
    planes, rows, cols = vel.shape[1:]
    total = None
    for y in range(0, rows, 8):
        for x in range(0, cols, 128):
            at = (slice(y, y + 8), slice(x, x + 128))
            w = [vel[(2, k) + at] for k in range(planes)]
            speed = [jnp.abs(w[k]) for k in range(planes)]
            for comp in range(3):
                u = w if comp == 2 else [vel[(comp, k) + at] for k in range(planes)]
                if comp < 2:
                    speed = [s + jnp.abs(v) for s, v in zip(speed, u)]
                flux = [a * b for a, b in zip(w, u)]
                for slot, field, root in ((comp, flux, R1), (3 + comp, u, R2)):
                    step = [field[k] - field[k - 1] for k in range(1, planes)]
                    up, down = step[0], step[-1]
                    for k in range(1, planes - 1):
                        up = step[k] + root * up
                        down = step[planes - 2 - k] + root * down
                    rightward[(slot,) + at] = up
                    leftward[(slot,) + at] = down
                rightward[(6 + comp,) + at] = u[planes - 1]
                leftward[(6 + comp,) + at] = u[0]
            for s in speed:
                total = s if total is None else jnp.maximum(total, s)
    peak[...] = jnp.broadcast_to(jnp.max(total, axis=0, keepdims=True), peak.shape)


def increment_kernel(vel, peaks, from_left, from_right, out):
    planes, rows, cols = vel.shape[1:]
    scale = COURANT / (jnp.max(peaks[...], keepdims=True) + 1e-06)
    gain1 = jnp.broadcast_to(A1 * scale, (8, 128))
    gain2 = jnp.broadcast_to(A2 * scale, (8, 128))
    for y in range(0, rows, 8):
        for x in range(0, cols, 128):
            at = (slice(y, y + 8), slice(x, x + 128))
            w = [vel[(2, k) + at] for k in range(planes)]
            w = [from_left[(8,) + at]] + w + [from_right[(8,) + at]]
            w1 = [gain1 * v for v in w]
            for comp in range(3):
                if comp == 2:
                    u = w
                else:
                    u = [vel[(comp, k) + at] for k in range(planes)]
                    u = [from_left[(6 + comp,) + at]] + u + [from_right[(6 + comp,) + at]]
                f1 = [a * b for a, b in zip(w1, u)]
                f2 = [gain2 * v for v in u]
                g1 = [f1[k + 1] - f1[k] for k in range(planes + 1)]
                g2 = [f2[k + 1] - f2[k] for k in range(planes + 1)]
                p1 = gain1 * from_left[(comp,) + at]
                p2 = gain2 * from_left[(3 + comp,) + at]
                forward = []
                for k in range(planes):
                    p1 = g1[k] + R1 * p1
                    p2 = g2[k] + R2 * p2
                    forward.append(p2 - p1)
                q1 = gain1 * from_right[(comp,) + at]
                q2 = gain2 * from_right[(3 + comp,) + at]
                for k in reversed(range(planes)):
                    q1 = g1[k + 1] + R1 * q1
                    q2 = g2[k + 1] + R2 * q2
                    near = (E1 / A1) * (g1[k] + g1[k + 1]) - (E2 / A2) * (g2[k] - g2[k + 1])
                    out[(comp, k) + at] = (forward[k] - (q1 + q2)) + near


def mesh_groups(shape, free):
    count = 1
    for size in shape:
        count *= size
    groups = {}
    for flat in range(count):
        rest, coords = flat, []
        for size in reversed(shape):
            coords.append(rest % size)
            rest //= size
        coords = coords[::-1]
        key = tuple(c for axis, c in enumerate(coords) if axis not in free)
        groups.setdefault(key, []).append(flat)
    return list(groups.values())


def spread(rows, axes, groups):
    return lax.all_to_all(rows, axes, 0, 0, tiled=True, axis_index_groups=groups)


def solution(mesh):
    axes = ("gz", "gy")
    slabs, lines = mesh.shape["gz"], mesh.shape["gy"]
    ring = 16
    shape = (slabs // (2 * ring), ring, 2, lines)
    across = mesh_groups(shape, (0, 2, 3))
    along = mesh_groups(shape, (1,))

    def body(velocity):
        _, planes, rows, cols = velocity.shape
        packet = jax.ShapeDtypeStruct((9, rows, cols), jnp.float32)
        n_across, n_along = len(across[0]), len(along[0])
        peak, rightward, leftward = pl.pallas_call(
            edges_kernel,
            out_shape=(jax.ShapeDtypeStruct((n_across, 128), jnp.float32), packet, packet),
            name="edges",
        )(velocity)
        from_left = lax.ppermute(rightward, "gz", [(i, (i + 1) % slabs) for i in range(slabs)])
        from_right = lax.ppermute(leftward, "gz", [(i, (i - 1) % slabs) for i in range(slabs)])
        peak = jnp.max(spread(peak, axes, across), axis=0, keepdims=True)
        peaks = spread(jnp.broadcast_to(peak, (n_along, 128)), axes, along)
        return pl.pallas_call(
            increment_kernel,
            out_shape=jax.ShapeDtypeStruct(velocity.shape, jnp.float32),
            name="increment",
        )(velocity, peaks, from_left, from_right)

    return jax.shard_map(
        body,
        mesh=mesh,
        in_specs=(P(None, "gz", "gy", None),),
        out_specs=P(None, "gz", "gy", None),
        check_vma=False,
    )
```

time: 166 us -> 63.4 us (0.38)
  blocking collectives: 119 us -> 39.4 us
  starting transfers between devices: 28.5 us -> 18 us
  waiting for transfers between devices: 8.07 us -> 0.01 us
  Pallas kernels: 0 us -> 4.92 us
  matrix products: 2.99 us -> 0 us
  local copies, waits for them, and re-layouts: 3.29 us -> 0.69 us
  other arithmetic: 2.51 us -> 0.08 us
    pmax x1 -> x0, blocking collectives: 119 us -> none  [body(): highest = lax.pmax(local_highest, ('gz', 'gy'))]
    all_to_all x0 -> x2, blocking collectives: none -> 39.4 us  [spread(): lax.all_to_all(rows, axes, 0, 0, tiled=True, axis_index_groups=groups)]
    ppermute x4 -> x2, starting transfers between devices: 28.5 us -> 18 us  [the longest x1 12.6 us: body(): lax.ppermute(leftward, 'gz', [(i, (i - 1) % slabs) for i in range(slabs)])]
    ppermute x4 -> x2, waiting for transfers between devices: 8.07 us -> 0.01 us  [the longest x1 0.01 us: body(): lax.ppermute(rightward, 'gz', [(i, (i + 1) % slabs) for i in range(slabs)])]
    pallas_call x0 -> x2, Pallas kernels: none -> 4.92 us  [the longest x1 2.81 us: body(): pl.pallas_call(increment_kernel, out_shape=jax.ShapeDtypeStruct(velocity....]
    dot_general x2 -> x0, matrix products: 2.99 us -> none  [cycle_pass(): jnp.einsum('sjm,smyx->sjyx', kernel_table, values, precision=lax.Precisio...]
  transfers between devices with their start and end apart: 4 -> 2, of which waited for: 2 -> 0; matrix products, arithmetic and copies ran while one was open for 1% -> 0% of each run, Pallas kernels for 0% -> 0%
where the time goes in v1:
time: 63.4 us; the launch traced here: 63.1 us
  blocking collectives  39.4 us (62%)
  starting transfers between devices  18 us (28%)
  Pallas kernels  4.92 us (8%)
  local copies, waits for them, and re-layouts  0.69 us (1%)
    all_to_all x2, blocking collectives, spread(): lax.all_to_all(rows, axes, 0, 0, tiled=True, axis_index_groups=groups)  39.4 us
    ppermute x1, starting transfers between devices, body(): lax.ppermute(leftward, 'gz', [(i, (i - 1) % slabs) for i in range(slabs)])  12.6 us
    ppermute x1, starting transfers between devices, body(): lax.ppermute(rightward, 'gz', [(i, (i + 1) % slabs) for i in range(slabs)])  5.38 us
    pallas_call x1, Pallas kernels, body(): pl.pallas_call(increment_kernel, out_shape=jax.ShapeDtypeStruct(velocity....  2.81 us
    pallas_call x1, Pallas kernels, body(): pl.pallas_call(edges_kernel, out_shape=(jax.ShapeDtypeStruct((n_across, 1...  2.12 us
  transfers between devices with their start and end apart: 2, of which 0 were waited for; matrix products, arithmetic and copies ran while one was open for 0% of the time, Pallas kernels for 0%

profile of v1, /device:TPU:1, one launch (start us, length us, event | category | flops | bytes accessed | tf_op | source)
XLA Modules:
  0.0 63.1 jit_solution(8272762018726950143)
XLA Ops:
  0.0 2.1 %edges.1 = (f32[64,128]{1,0:T(8,128)}, f32[9,16,256]{2,1,0:T(8,128)}, f32[9,16,256]{2,1,0:T(8,128)}) custom-call(f32[3,16,16,256]{3,2,1,0:T(8,128)} %vel.3), custom_call_target="tpu_custom_call" | custom-call | tf_op jit(solution)/shard_map/edges/pallas_call | solution.py:131
  2.1 5.4 %collective-permute-start = (f32[9,16,256]{2,1,0:T(8,128)}, f32[9,16,256]{2,1,0:T(8,128)S(1)}, u32[]{:S(2)}, u32[]{:S(2)}) collective-permute-start(f32[9,16,256]{2,1,0:T(8,128)} %get-tuple-element.9), channel_id=1, source_target_pairs={{0,8},{8,16},{16,24},{24,32},{32,40},{40,48},{48,56},{56,64},{64,7... | collective-permute-start | bytes 442376 | tf_op jit(solution)/shard_map/ppermute | solution.py:136
  7.5 12.6 %collective-permute-start.1 = (f32[9,16,256]{2,1,0:T(8,128)}, f32[9,16,256]{2,1,0:T(8,128)S(1)}, u32[]{:S(2)}, u32[]{:S(2)}) collective-permute-start(f32[9,16,256]{2,1,0:T(8,128)} %get-tuple-element.10), channel_id=1, source_target_pairs={{0,1016},{8,0},{16,8},{24,16},{32,24},{40,32},{48,40},{56,48},{64,... | collective-permute-start | bytes 442376 | tf_op jit(solution)/shard_map/ppermute | solution.py:137
  20.1 22.5 %all_to_all.17 = f32[64,1,128]{2,1,0:T(1,128)S(1)} all-to-all(f32[64,1,128]{2,1,0:T(1,128)} %bitcast.5), channel_id=1, replica_groups={{0,1,2,3,4,5,6,7,8,9,10,11,12,13,14,15,256,257,258,259,260,261,262,263,..., dimensions={0} | all-to-all | bytes 65536 | tf_op jit(solution)/shard_map/all_to_all | solution.py:116
  42.6 0.1 reduce_max.9
  42.7 16.9 %all_to_all.18 = f32[16,1,128]{2,1,0:T(1,128)} all-to-all(f32[16,1,128]{2,1,0:T(1,128)S(1)} %broadcast_in_dim.2), channel_id=1, replica_groups={{0,16,32,48,64,80,96,112,128,144,160,176,192,208,224,240},{1,17,33,49,6..., dimensions={0} | all-to-all | bytes 16384 | tf_op jit(solution)/shard_map/all_to_all | solution.py:116
  59.6 0.0 collective-permute-done.from_left
  59.6 0.0 copy-start
  59.6 0.0 collective-permute-done.1.from_right
  59.6 0.0 copy-start.1
  59.6 0.6 %copy-done = f32[9,16,256]{2,1,0:T(8,128)} copy-done((f32[9,16,256]{2,1,0:T(8,128)}, f32[9,16,256]{2,1,0:T(8,128)S(1)}, u32[]{:S(2)}) %copy-start) | copy-done | bytes 147480
  60.3 0.0 copy-done.1
  60.3 2.8 %increment.1 = f32[3,16,16,256]{3,2,1,0:T(8,128)} custom-call(f32[3,16,16,256]{3,2,1,0:T(8,128)} %vel.3, f32[16,128]{1,0:T(8,128)} %bitcast.4, f32[9,16,256]{2,1,0:T(8,128)} %copy-done, f32[9,16,256]{2,1,0:T(8,128)} %copy-done.1), custom_call_target="tpu_custom_call" | custom-call | tf_op jit(solution)/shard_map/increment/pallas_call | solution.py:140
  (1 shorter events, 0.0 us)
Async XLA Ops:
  2.1 57.5 %collective-permute-start = (f32[9,16,256]{2,1,0:T(8,128)}, f32[9,16,256]{2,1,0:T(8,128)S(1)}, u32[]{:S(2)}, u32[]{:S(2)}) collective-permute-start(f32[9,16,256]{2,1,0:T(8,128)} %get-tuple-element.9), channel_id=1, source_target_pairs={{0,8},{8,16},{16,24},{24,32},{32,40},{40,48},{48,56},{56,64},{64,7... | collective-permute-start | bytes 442376 | tf_op jit(solution)/shard_map/ppermute | solution.py:136
  7.5 52.1 %collective-permute-start.1 = (f32[9,16,256]{2,1,0:T(8,128)}, f32[9,16,256]{2,1,0:T(8,128)S(1)}, u32[]{:S(2)}, u32[]{:S(2)}) collective-permute-start(f32[9,16,256]{2,1,0:T(8,128)} %get-tuple-element.10), channel_id=1, source_target_pairs={{0,1016},{8,0},{16,8},{24,16},{32,24},{40,32},{48,40},{56,48},{64,... | collective-permute-start | bytes 442376 | tf_op jit(solution)/shard_map/ppermute | solution.py:137
  59.6 0.7 %copy-start = (f32[9,16,256]{2,1,0:T(8,128)}, f32[9,16,256]{2,1,0:T(8,128)S(1)}, u32[]{:S(2)}) copy-start(f32[9,16,256]{2,1,0:T(8,128)S(1)} %collective-permute-done.from_left) | copy-start | bytes 442372
  59.6 0.7 %copy-start.1 = (f32[9,16,256]{2,1,0:T(8,128)}, f32[9,16,256]{2,1,0:T(8,128)S(1)}, u32[]{:S(2)}) copy-start(f32[9,16,256]{2,1,0:T(8,128)S(1)} %collective-permute-done.1.from_right) | copy-start | bytes 442372

commit v2 on v1

v2 whole, which is shorter than its diff:
```python
import jax
import jax.numpy as jnp
from jax import lax
from jax.experimental import pallas as pl
from jax.experimental.pallas import tpu as pltpu
from jax.sharding import PartitionSpec as P

COURANT = 4.0
FIRST_ROOT = -0.38196601125010515
SECOND_ROOT = -0.18826230851010056
FIRST_OFF, FIRST_NEAR, FIRST_FAR = 1.0 / 3.0, 7.0 / 9.0, 1.0 / 36.0
SECOND_OFF, SECOND_NEAR, SECOND_FAR = 2.0 / 11.0, 12.0 / 11.0, 3.0 / 44.0


def filter_constants():
    r = FIRST_ROOT
    gain = 1.0 / (1.0 + 2.0 * FIRST_OFF * r)
    tail = gain * (FIRST_NEAR * (r - 1.0 / r) + FIRST_FAR * (r * r - 1.0 / (r * r)))
    first = (r, -tail * r / (1.0 - r), -gain * FIRST_FAR * (r - 1.0 / r))
    r = SECOND_ROOT
    gain = 1.0 / (1.0 + 2.0 * SECOND_OFF * r)
    tail = gain * (
        SECOND_NEAR * (r + 1.0 / r)
        + SECOND_FAR * (r * r + 1.0 / (r * r))
        - 2.0 * (SECOND_NEAR + SECOND_FAR)
    )
    second = (r, -tail * r / (1.0 - r), gain * SECOND_FAR * (r - 1.0 / r))
    return first, second


(R1, A1, E1), (R2, A2, E2) = filter_constants()


def columns(rows, cols):
    return [(slice(y, y + 8), slice(x, x + 128)) for y in range(0, rows, 8) for x in range(0, cols, 128)]


def peak_kernel(vel, peak):
    planes, rows, cols = vel.shape[1:]
    total = None
    for at in columns(rows, cols):
        for k in range(planes):
            speed = sum(jnp.abs(vel[(comp, k) + at]) for comp in range(3))
            total = speed if total is None else jnp.maximum(total, speed)
    peak[...] = jnp.broadcast_to(jnp.max(total, axis=0, keepdims=True), peak.shape)


def edges_kernel(vel, rightward, leftward):
    planes, rows, cols = vel.shape[1:]
    for at in columns(rows, cols):
        w = [vel[(2, k) + at] for k in range(planes)]
        for comp in range(3):
            u = w if comp == 2 else [vel[(comp, k) + at] for k in range(planes)]
            flux = [a * b for a, b in zip(w, u)]
            for slot, field, root in ((comp, flux, R1), (3 + comp, u, R2)):
                step = [field[k] - field[k - 1] for k in range(1, planes)]
                up, down = step[0], step[-1]
                for k in range(1, planes - 1):
                    up = step[k] + root * up
                    down = step[planes - 2 - k] + root * down
                rightward[(slot,) + at] = up
                leftward[(slot,) + at] = down
            rightward[(6 + comp,) + at] = u[planes - 1]
            leftward[(6 + comp,) + at] = u[0]


def tendency_kernel(vel, from_left, from_right, _, out):
    planes, rows, cols = vel.shape[1:]
    for at in columns(rows, cols):
        w = [vel[(2, k) + at] for k in range(planes)]
        w = [from_left[(8,) + at]] + w + [from_right[(8,) + at]]
        w1 = [A1 * v for v in w]
        for comp in range(3):
            if comp == 2:
                u = w
            else:
                u = [vel[(comp, k) + at] for k in range(planes)]
                u = [from_left[(6 + comp,) + at]] + u + [from_right[(6 + comp,) + at]]
            f1 = [a * b for a, b in zip(w1, u)]
            f2 = [A2 * v for v in u]
            g1 = [f1[k + 1] - f1[k] for k in range(planes + 1)]
            g2 = [f2[k + 1] - f2[k] for k in range(planes + 1)]
            p1 = A1 * from_left[(comp,) + at]
            p2 = A2 * from_left[(3 + comp,) + at]
            forward = []
            for k in range(planes):
                p1 = g1[k] + R1 * p1
                p2 = g2[k] + R2 * p2
                forward.append(p2 - p1)
            q1 = A1 * from_right[(comp,) + at]
            q2 = A2 * from_right[(3 + comp,) + at]
            for k in reversed(range(planes)):
                q1 = g1[k + 1] + R1 * q1
                q2 = g2[k + 1] + R2 * q2
                near = (E1 / A1) * (g1[k] + g1[k + 1]) - (E2 / A2) * (g2[k] - g2[k + 1])
                out[(comp, k) + at] = (forward[k] - (q1 + q2)) + near


def scale_kernel(tendency, peaks, out):
    scale = COURANT / (jnp.max(peaks[...], keepdims=True) + 1e-06)
    out[...] = tendency[...] * jnp.broadcast_to(scale.reshape(1, 1, 1, 1), tendency.shape)


def mesh_groups(shape, free):
    count = 1
    for size in shape:
        count *= size
    groups = {}
    for flat in range(count):
        rest, coords = flat, []
        for size in reversed(shape):
            coords.append(rest % size)
            rest //= size
        coords = coords[::-1]
        key = tuple(c for axis, c in enumerate(coords) if axis not in free)
        groups.setdefault(key, []).append(flat)
    return list(groups.values())


def spread(rows, axes, groups):
    return lax.all_to_all(rows, axes, 0, 0, tiled=True, axis_index_groups=groups)


def work(micros):
    return pl.CostEstimate(flops=int(micros * 1e6), bytes_accessed=int(micros * 3e6), transcendentals=0)


def in_vmem(array):
    return pltpu.with_memory_space_constraint(array, pltpu.VMEM)


def solution(mesh):
    axes = ("gz", "gy")
    slabs, lines = mesh.shape["gz"], mesh.shape["gy"]
    ring = 16
    shape = (slabs // (2 * ring), ring, 2, lines)
    across = mesh_groups(shape, (0, 2, 3))
    along = mesh_groups(shape, (1,))

    def body(velocity):
        _, planes, rows, cols = velocity.shape
        n_across, n_along = len(across[0]), len(along[0])
        local = pl.BlockSpec(memory_space=pltpu.VMEM)
        held = in_vmem(velocity)
        packet = pltpu.VMEM((9, rows, cols), jnp.float32)
        peak = pl.pallas_call(
            peak_kernel,
            out_shape=pltpu.VMEM((n_across, 128), jnp.float32),
            in_specs=[local],
            out_specs=local,
            cost_estimate=work(0.3),
            name="peak",
        )(held)
        rightward, leftward = pl.pallas_call(
            edges_kernel,
            out_shape=(packet, packet),
            in_specs=[local],
            out_specs=(local, local),
            cost_estimate=work(1.0),
            name="edges",
        )(held)
        from_left = in_vmem(lax.ppermute(rightward, "gz", [(i, (i + 1) % slabs) for i in range(slabs)]))
        from_right = in_vmem(lax.ppermute(leftward, "gz", [(i, (i - 1) % slabs) for i in range(slabs)]))
        peak = jnp.max(spread(peak, axes, across), axis=0, keepdims=True)
        peak = jnp.broadcast_to(peak, (n_along, 128))
        peaks = in_vmem(spread(peak, axes, along))
        tendency = pl.pallas_call(
            tendency_kernel,
            out_shape=pltpu.VMEM(velocity.shape, jnp.float32),
            in_specs=[local] * 4,
            out_specs=local,
            cost_estimate=work(1.0),
            name="tendency",
        )(held, from_left, from_right, in_vmem(peak))
        return pl.pallas_call(
            scale_kernel,
            out_shape=jax.ShapeDtypeStruct(velocity.shape, jnp.float32),
            in_specs=[local, local],
            name="scale",
        )(in_vmem(tendency), peaks)

    return jax.shard_map(
        body,
        mesh=mesh,
        in_specs=(P(None, "gz", "gy", None),),
        out_specs=P(None, "gz", "gy", None),
        check_vma=False,
    )
```

time: 63.4 us -> 60.8 us (0.959)
  blocking collectives: 39.4 us -> 22.2 us
  waiting for transfers between devices: 0.01 us -> 10.6 us
  starting transfers between devices: 18 us -> 23.7 us
  Pallas kernels: 4.92 us -> 2.06 us
  local copies, waits for them, and re-layouts: 0.69 us -> 1.74 us
    all_to_all x2 -> x1, blocking collectives: 39.4 us -> 22.2 us  [spread(): lax.all_to_all(rows, axes, 0, 0, tiled=True, axis_index_groups=groups)]
    all_to_all x0 -> x1, waiting for transfers between devices: none -> 10.6 us  [spread(): lax.all_to_all(rows, axes, 0, 0, tiled=True, axis_index_groups=groups)]
    all_to_all x0 -> x1, starting transfers between devices: none -> 5.74 us  [spread(): lax.all_to_all(rows, axes, 0, 0, tiled=True, axis_index_groups=groups)]
    pallas_call x2 -> x4, Pallas kernels: 4.92 us -> 2.06 us  [the longest x1 1.06 us: body(): pl.pallas_call(scale_kernel, out_shape=jax.ShapeDtypeStruct(velocity.shap...]
  transfers between devices with their start and end apart: 2 -> 3, of which waited for: 0 -> 1; matrix products, arithmetic and copies ran while one was open for 0% -> 1% of each run, Pallas kernels for 0% -> 1%
where the time goes in v2:
time: 60.8 us; the launch traced here: 60.5 us
  starting transfers between devices  23.7 us (39%)
  blocking collectives  22.2 us (37%)
  waiting for transfers between devices  10.6 us (17%)
  Pallas kernels  2.06 us (3%)
  local copies, waits for them, and re-layouts  1.74 us (3%)
    all_to_all x1, blocking collectives, spread(): lax.all_to_all(rows, axes, 0, 0, tiled=True, axis_index_groups=groups)  22.2 us
    ppermute x1, starting transfers between devices, body(): lax.ppermute(leftward, 'gz', [(i, (i - 1) % slabs) for i in range(slabs)])  12.6 us
    all_to_all x1, waiting for transfers between devices, spread(): lax.all_to_all(rows, axes, 0, 0, tiled=True, axis_index_groups=groups)  10.6 us
    all_to_all x1, starting transfers between devices, spread(): lax.all_to_all(rows, axes, 0, 0, tiled=True, axis_index_groups=groups)  5.74 us
    ppermute x1, starting transfers between devices, body(): lax.ppermute(rightward, 'gz', [(i, (i + 1) % slabs) for i in range(slabs)])  5.39 us
  transfers between devices with their start and end apart: 3, of which 1 were waited for; matrix products, arithmetic and copies ran while one was open for 1% of the time, Pallas kernels for 1%

profile of v2, /device:TPU:1, one launch (start us, length us, event | category | flops | bytes accessed | tf_op | source)
XLA Modules:
  0.0 60.5 jit_solution(13839896161369363423)
XLA Ops:
  0.0 0.0 copy-start
  0.0 1.1 %copy-done = f32[3,16,16,256]{3,2,1,0:T(8,128)S(1)} copy-done((f32[3,16,16,256]{3,2,1,0:T(8,128)S(1)}, f32[3,16,16,256]{3,2,1,0:T(8,128)}, u32[]{:S(2)}) %copy-start) | copy-done | bytes 786456
  1.1 0.3 edges.1
  1.4 5.4 %collective-permute-start = (f32[9,16,256]{2,1,0:T(8,128)S(1)}, f32[9,16,256]{2,1,0:T(8,128)S(1)}, u32[]{:S(2)}, u32[]{:S(2)}) collective-permute-start(f32[9,16,256]{2,1,0:T(8,128)S(1)} %get-tuple-element.7), channel_id=1, source_target_pairs={{0,8},{8,16},{16,24},{24,32},{32,40},{40,48},{48,56},{56,64},{64,7... | collective-permute-start | bytes 442376 | tf_op jit(solution)/shard_map/ppermute | solution.py:162
  6.8 12.6 %collective-permute-start.1 = (f32[9,16,256]{2,1,0:T(8,128)S(1)}, f32[9,16,256]{2,1,0:T(8,128)S(1)}, u32[]{:S(2)}, u32[]{:S(2)}) collective-permute-start(f32[9,16,256]{2,1,0:T(8,128)S(1)} %get-tuple-element.8), channel_id=1, source_target_pairs={{0,1016},{8,0},{16,8},{24,16},{32,24},{40,32},{48,40},{56,48},{64,... | collective-permute-start | bytes 442376 | tf_op jit(solution)/shard_map/ppermute | solution.py:163
  19.4 0.1 peak.1
  19.5 22.2 %all_to_all.17 = f32[64,1,128]{2,1,0:T(1,128)S(1)} all-to-all(f32[64,1,128]{2,1,0:T(1,128)S(1)} %bitcast.4), channel_id=1, replica_groups={{0,1,2,3,4,5,6,7,8,9,10,11,12,13,14,15,256,257,258,259,260,261,262,263,..., dimensions={0} | all-to-all | bytes 65536 | tf_op jit(solution)/shard_map/all_to_all | solution.py:121
  41.7 0.1 reduce_max.9
  41.8 0.6 %broadcast_in_dim.9 = f32[16,1,128]{2,1,0:T(1,128)} broadcast(f32[128]{0:T(128)S(1)} %reduce_max.9), dimensions={2} | broadcast | bytes 8704 | tf_op jit(solution)/shard_map/broadcast_in_dim | solution.py:165
  42.4 5.7 %all-to-all-start.1 = ((f32[16,1,128]{2,1,0:T(1,128)}), f32[16,1,128]{2,1,0:T(1,128)S(1)}, u32[]{:S(2)}, u32[]{:S(2)}) async-start(f32[16,1,128]{2,1,0:T(1,128)} %broadcast_in_dim.9), calls=%async_computation.1 | async-start | bytes 16384 | tf_op jit(solution)/shard_map/all_to_all | solution.py:121
  48.2 0.0 collective-permute-done.from_left
  48.2 0.0 collective-permute-done.1.from_right
  48.2 0.6 %tendency.1 = f32[3,16,16,256]{3,2,1,0:T(8,128)S(1)} custom-call(f32[3,16,16,256]{3,2,1,0:T(8,128)S(1)} %copy-done, f32[9,16,256]{2,1,0:T(8,128)S(1)} %collective-permute-done.from_left, f32[9,16,256]{2,1,0:T(8,128)S(1)} %collective-permute-done.1.from_right, f32[16,128]{1,0:T(8,128)S(1)} %broadcast_in_dim.8._), custom_call_target="tpu_custom_call" | custom-call | flops 1000000 | bytes 3000000 | tf_op jit(solution)/shard_map/tendency/pallas_call | solution.py:167
  48.8 10.6 %all-to-all-done.1 = f32[16,1,128]{2,1,0:T(1,128)S(1)} async-done(((f32[16,1,128]{2,1,0:T(1,128)}), f32[16,1,128]{2,1,0:T(1,128)S(1)}, u32[]{:S(2)}, u32[]{:S(2)}) %all-to-all-start.1) | async-done | bytes 8224 | tf_op jit(solution)/shard_map/all_to_all | solution.py:121
  59.4 1.1 %scale.1 = f32[3,16,16,256]{3,2,1,0:T(8,128)} custom-call(f32[3,16,16,256]{3,2,1,0:T(8,128)S(1)} %tendency.1, f32[16,128]{1,0:T(8,128)S(1)} %bitcast.5), custom_call_target="tpu_custom_call" | custom-call | tf_op jit(solution)/shard_map/scale/pallas_call | solution.py:175
  (1 shorter events, 0.0 us)
Async XLA Ops:
  0.0 1.1 %copy-start = (f32[3,16,16,256]{3,2,1,0:T(8,128)S(1)}, f32[3,16,16,256]{3,2,1,0:T(8,128)}, u32[]{:S(2)}) copy-start(f32[3,16,16,256]{3,2,1,0:T(8,128)} %vel.5) | copy-start | bytes 2359300
  1.4 46.8 %collective-permute-start = (f32[9,16,256]{2,1,0:T(8,128)S(1)}, f32[9,16,256]{2,1,0:T(8,128)S(1)}, u32[]{:S(2)}, u32[]{:S(2)}) collective-permute-start(f32[9,16,256]{2,1,0:T(8,128)S(1)} %get-tuple-element.7), channel_id=1, source_target_pairs={{0,8},{8,16},{16,24},{24,32},{32,40},{40,48},{48,56},{56,64},{64,7... | collective-permute-start | bytes 442376 | tf_op jit(solution)/shard_map/ppermute | solution.py:162
  6.8 41.4 %collective-permute-start.1 = (f32[9,16,256]{2,1,0:T(8,128)S(1)}, f32[9,16,256]{2,1,0:T(8,128)S(1)}, u32[]{:S(2)}, u32[]{:S(2)}) collective-permute-start(f32[9,16,256]{2,1,0:T(8,128)S(1)} %get-tuple-element.8), channel_id=1, source_target_pairs={{0,1016},{8,0},{16,8},{24,16},{32,24},{40,32},{48,40},{56,48},{64,... | collective-permute-start | bytes 442376 | tf_op jit(solution)/shard_map/ppermute | solution.py:163
  42.4 17.0 %all-to-all-start.1 = ((f32[16,1,128]{2,1,0:T(1,128)}), f32[16,1,128]{2,1,0:T(1,128)S(1)}, u32[]{:S(2)}, u32[]{:S(2)}) async-start(f32[16,1,128]{2,1,0:T(1,128)} %broadcast_in_dim.9), calls=%async_computation.1 | async-start | bytes 16384 | tf_op jit(solution)/shard_map/all_to_all | solution.py:121

commit v3 on v2

--- a/solution.py
+++ b/solution.py
@@ -43,6 +43,10 @@
             speed = sum(jnp.abs(vel[(comp, k) + at]) for comp in range(3))
             total = speed if total is None else jnp.maximum(total, speed)
     peak[...] = jnp.broadcast_to(jnp.max(total, axis=0, keepdims=True), peak.shape)
+
+
+def merge_kernel(peaks, peak):
+    peak[...] = jnp.broadcast_to(jnp.max(peaks[...], axis=0, keepdims=True), peak.shape)
 
 
 def edges_kernel(vel, rightward, leftward):
@@ -122,7 +126,7 @@
 
 
 def work(micros):
-    return pl.CostEstimate(flops=int(micros * 1e6), bytes_accessed=int(micros * 3e6), transcendentals=0)
+    return pl.CostEstimate(flops=int(micros * 1e9), bytes_accessed=int(micros * 3e6), transcendentals=0)
 
 
 def in_vmem(array):
@@ -156,22 +160,28 @@
             out_shape=(packet, packet),
             in_specs=[local],
             out_specs=(local, local),
-            cost_estimate=work(1.0),
+            cost_estimate=work(5),
             name="edges",
         )(held)
         from_left = in_vmem(lax.ppermute(rightward, "gz", [(i, (i + 1) % slabs) for i in range(slabs)]))
         from_right = in_vmem(lax.ppermute(leftward, "gz", [(i, (i - 1) % slabs) for i in range(slabs)]))
-        peak = jnp.max(spread(peak, axes, across), axis=0, keepdims=True)
-        peak = jnp.broadcast_to(peak, (n_along, 128))
-        peaks = in_vmem(spread(peak, axes, along))
+        merged = pl.pallas_call(
+            merge_kernel,
+            out_shape=pltpu.VMEM((n_along, 128), jnp.float32),
+            in_specs=[local],
+            out_specs=local,
+            cost_estimate=work(1),
+            name="merge",
+        )(in_vmem(spread(peak, axes, across)))
+        peaks = in_vmem(spread(in_vmem(merged), axes, along))
         tendency = pl.pallas_call(
             tendency_kernel,
             out_shape=pltpu.VMEM(velocity.shape, jnp.float32),
             in_specs=[local] * 4,
             out_specs=local,
-            cost_estimate=work(1.0),
+            cost_estimate=work(1),
             name="tendency",
-        )(held, from_left, from_right, in_vmem(peak))
+        )(held, from_left, from_right, in_vmem(merged))
         return pl.pallas_call(
             scale_kernel,
             out_shape=jax.ShapeDtypeStruct(velocity.shape, jnp.float32),

time: 60.8 us -> 54.4 us (0.89)
  blocking collectives: 22.2 us -> 0 us
  starting transfers between devices: 23.7 us -> 34.5 us
  waiting for transfers between devices: 10.6 us -> 14.4 us
  Pallas kernels: 2.06 us -> 4.01 us
    all_to_all x1 -> x2, starting transfers between devices: 5.74 us -> 30.1 us  [spread(): lax.all_to_all(rows, axes, 0, 0, tiled=True, axis_index_groups=groups)]
    all_to_all x1 -> x0, blocking collectives: 22.2 us -> none  [spread(): lax.all_to_all(rows, axes, 0, 0, tiled=True, axis_index_groups=groups)]
    ppermute x1, starting transfers between devices: 12.6 us -> 2.43 us  [body(): lax.ppermute(leftward, 'gz', [(i, (i - 1) % slabs) for i in range(slabs)])]
    all_to_all x1 -> x2, waiting for transfers between devices: 10.6 us -> 14.4 us  [spread(): lax.all_to_all(rows, axes, 0, 0, tiled=True, axis_index_groups=groups)]
    ppermute x1, starting transfers between devices: 5.39 us -> 1.92 us  [body(): lax.ppermute(rightward, 'gz', [(i, (i + 1) % slabs) for i in range(slabs)])]
    pallas_call x1, Pallas kernels: 0.62 us -> 1.35 us  [body(): pl.pallas_call(tendency_kernel, out_shape=pltpu.VMEM(velocity.shape, jnp....]
    pallas_call x1, Pallas kernels: 0.09 us -> 0.7 us  [body(): pl.pallas_call(peak_kernel, out_shape=pltpu.VMEM((n_across, 128), jnp.flo...]
    pallas_call x0 -> x1, Pallas kernels: none -> 0.61 us  [body(): pl.pallas_call(merge_kernel, out_shape=pltpu.VMEM((n_along, 128), jnp.flo...]
  transfers between devices with their start and end apart: 3 -> 4, of which waited for: 1 -> 2; matrix products, arithmetic and copies ran while one was open for 1% -> 0% of each run, Pallas kernels for 1% -> 4%
where the time goes in v3:
time: 54.4 us; the launch traced here: 54.1 us
  starting transfers between devices  34.5 us (63%)
  waiting for transfers between devices  14.4 us (26%)
  Pallas kernels  4.01 us (7%)
  local copies, waits for them, and re-layouts  1.14 us (2%)
    all_to_all x2, starting transfers between devices, spread(): lax.all_to_all(rows, axes, 0, 0, tiled=True, axis_index_groups=groups)  30.1 us
    all_to_all x2, waiting for transfers between devices, spread(): lax.all_to_all(rows, axes, 0, 0, tiled=True, axis_index_groups=groups)  14.4 us
    ppermute x1, starting transfers between devices, body(): lax.ppermute(leftward, 'gz', [(i, (i - 1) % slabs) for i in range(slabs)])  2.43 us
    ppermute x1, starting transfers between devices, body(): lax.ppermute(rightward, 'gz', [(i, (i + 1) % slabs) for i in range(slabs)])  1.92 us
    pallas_call x1, Pallas kernels, body(): pl.pallas_call(tendency_kernel, out_shape=pltpu.VMEM(velocity.shape, jnp....  1.35 us
    unnamed x4, local copies, waits for them, and re-layouts  1.14 us
  transfers between devices with their start and end apart: 4, of which 2 were waited for; matrix products, arithmetic and copies ran while one was open for 0% of the time, Pallas kernels for 4%

profile of v3, /device:TPU:1, one launch (start us, length us, event | category | flops | bytes accessed | tf_op | source)
XLA Modules:
  0.0 54.1 jit_solution(8731329981624823741)
XLA Ops:
  0.0 0.0 copy-start
  0.0 1.1 %copy-done = f32[3,16,16,256]{3,2,1,0:T(8,128)S(1)} copy-done((f32[3,16,16,256]{3,2,1,0:T(8,128)S(1)}, f32[3,16,16,256]{3,2,1,0:T(8,128)}, u32[]{:S(2)}) %copy-start) | copy-done | bytes 786456
  1.1 0.7 %peak.1 = f32[64,128]{1,0:T(8,128)} custom-call(f32[3,16,16,256]{3,2,1,0:T(8,128)S(1)} %copy-done), custom_call_target="tpu_custom_call" | custom-call | flops 300000000 | bytes 900000 | tf_op jit(solution)/shard_map/peak/pallas_call | solution.py:150
  1.8 18.2 %all-to-all-start = ((f32[64,1,128]{2,1,0:T(1,128)}), f32[64,1,128]{2,1,0:T(1,128)S(1)}, u32[]{:S(2)}, u32[]{:S(2)}) async-start(f32[64,1,128]{2,1,0:T(1,128)} %bitcast.1), calls=%async_computation | async-start | bytes 65536 | tf_op jit(solution)/shard_map/all_to_all | solution.py:125
  20.1 0.3 edges.1
  20.4 1.9 %collective-permute-start = (f32[9,16,256]{2,1,0:T(8,128)S(1)}, f32[9,16,256]{2,1,0:T(8,128)S(1)}, u32[]{:S(2)}, u32[]{:S(2)}) collective-permute-start(f32[9,16,256]{2,1,0:T(8,128)S(1)} %get-tuple-element.7), channel_id=1, source_target_pairs={{0,8},{8,16},{16,24},{24,32},{32,40},{40,48},{48,56},{56,64},{64,7... | collective-permute-start | bytes 442376 | tf_op jit(solution)/shard_map/ppermute | solution.py:166
  22.3 2.4 %collective-permute-start.1 = (f32[9,16,256]{2,1,0:T(8,128)S(1)}, f32[9,16,256]{2,1,0:T(8,128)S(1)}, u32[]{:S(2)}, u32[]{:S(2)}) collective-permute-start(f32[9,16,256]{2,1,0:T(8,128)S(1)} %get-tuple-element.8), channel_id=1, source_target_pairs={{0,1016},{8,0},{16,8},{24,16},{32,24},{40,32},{48,40},{56,48},{64,... | collective-permute-start | bytes 442376 | tf_op jit(solution)/shard_map/ppermute | solution.py:167
  24.7 4.5 %all-to-all-done = f32[64,1,128]{2,1,0:T(1,128)S(1)} async-done(((f32[64,1,128]{2,1,0:T(1,128)}), f32[64,1,128]{2,1,0:T(1,128)S(1)}, u32[]{:S(2)}, u32[]{:S(2)}) %all-to-all-start) | async-done | bytes 32800 | tf_op jit(solution)/shard_map/all_to_all | solution.py:125
  29.3 0.0 copy-start.1
  29.3 0.6 %merge.1._ = f32[16,128]{1,0:T(8,128)} custom-call(f32[64,128]{1,0:T(8,128)S(1)} %bitcast.9), custom_call_target="tpu_custom_call" | custom-call | flops 1000000000 | bytes 3000000 | tf_op jit(solution)/shard_map/merge/pallas_call | solution.py:168
  29.9 11.9 %all-to-all-start.1 = ((f32[16,1,128]{2,1,0:T(1,128)}), f32[16,1,128]{2,1,0:T(1,128)S(1)}, u32[]{:S(2)}, u32[]{:S(2)}) async-start(f32[16,1,128]{2,1,0:T(1,128)} %bitcast.4), calls=%async_computation.1 | async-start | bytes 16384 | tf_op jit(solution)/shard_map/all_to_all | solution.py:125
  41.8 0.0 collective-permute-done.from_left
  41.8 0.0 collective-permute-done.1.from_right
  41.8 0.0 copy-done.1
  41.8 1.3 %tendency.1 = f32[3,16,16,256]{3,2,1,0:T(8,128)S(1)} custom-call(f32[3,16,16,256]{3,2,1,0:T(8,128)S(1)} %copy-done.1, f32[9,16,256]{2,1,0:T(8,128)S(1)} %collective-permute-done.from_left, f32[9,16,256]{2,1,0:T(8,128)S(1)} %collective-permute-done.1.from_right, f32[16,128]{1,0:T(8,128)} %merge.1._), custom_call_target="tpu_custom_call" | custom-call | flops 1000000000 | bytes 3000000 | tf_op jit(solution)/shard_map/tendency/pallas_call | solution.py:177
  43.2 9.8 %all-to-all-done.1 = f32[16,1,128]{2,1,0:T(1,128)S(1)} async-done(((f32[16,1,128]{2,1,0:T(1,128)}), f32[16,1,128]{2,1,0:T(1,128)S(1)}, u32[]{:S(2)}, u32[]{:S(2)}) %all-to-all-start.1) | async-done | bytes 8224 | tf_op jit(solution)/shard_map/all_to_all | solution.py:125
  53.0 1.1 %scale.1 = f32[3,16,16,256]{3,2,1,0:T(8,128)} custom-call(f32[3,16,16,256]{3,2,1,0:T(8,128)S(1)} %tendency.1, f32[16,128]{1,0:T(8,128)S(1)} %bitcast.8), custom_call_target="tpu_custom_call" | custom-call | tf_op jit(solution)/shard_map/scale/pallas_call | solution.py:185
Async XLA Ops:
  0.0 1.1 %copy-start = (f32[3,16,16,256]{3,2,1,0:T(8,128)S(1)}, f32[3,16,16,256]{3,2,1,0:T(8,128)}, u32[]{:S(2)}) copy-start(f32[3,16,16,256]{3,2,1,0:T(8,128)} %vel.5) | copy-start | bytes 2359300
  1.8 27.4 %all-to-all-start = ((f32[64,1,128]{2,1,0:T(1,128)}), f32[64,1,128]{2,1,0:T(1,128)S(1)}, u32[]{:S(2)}, u32[]{:S(2)}) async-start(f32[64,1,128]{2,1,0:T(1,128)} %bitcast.1), calls=%async_computation | async-start | bytes 65536 | tf_op jit(solution)/shard_map/all_to_all | solution.py:125
  20.4 21.4 %collective-permute-start = (f32[9,16,256]{2,1,0:T(8,128)S(1)}, f32[9,16,256]{2,1,0:T(8,128)S(1)}, u32[]{:S(2)}, u32[]{:S(2)}) collective-permute-start(f32[9,16,256]{2,1,0:T(8,128)S(1)} %get-tuple-element.7), channel_id=1, source_target_pairs={{0,8},{8,16},{16,24},{24,32},{32,40},{40,48},{48,56},{56,64},{64,7... | collective-permute-start | bytes 442376 | tf_op jit(solution)/shard_map/ppermute | solution.py:166
  22.3 19.5 %collective-permute-start.1 = (f32[9,16,256]{2,1,0:T(8,128)S(1)}, f32[9,16,256]{2,1,0:T(8,128)S(1)}, u32[]{:S(2)}, u32[]{:S(2)}) collective-permute-start(f32[9,16,256]{2,1,0:T(8,128)S(1)} %get-tuple-element.8), channel_id=1, source_target_pairs={{0,1016},{8,0},{16,8},{24,16},{32,24},{40,32},{48,40},{56,48},{64,... | collective-permute-start | bytes 442376 | tf_op jit(solution)/shard_map/ppermute | solution.py:167
  29.3 12.6 %copy-start.1 = (f32[3,16,16,256]{3,2,1,0:T(8,128)S(1)}, f32[3,16,16,256]{3,2,1,0:T(8,128)}, u32[]{:S(2)}) copy-start(f32[3,16,16,256]{3,2,1,0:T(8,128)} %vel.5) | copy-start | bytes 2359300
  29.9 23.1 %all-to-all-start.1 = ((f32[16,1,128]{2,1,0:T(1,128)}), f32[16,1,128]{2,1,0:T(1,128)S(1)}, u32[]{:S(2)}, u32[]{:S(2)}) async-start(f32[16,1,128]{2,1,0:T(1,128)} %bitcast.4), calls=%async_computation.1 | async-start | bytes 16384 | tf_op jit(solution)/shard_map/all_to_all | solution.py:125

commit v4 on v3

--- a/solution.py
+++ b/solution.py
@@ -35,13 +35,22 @@
     return [(slice(y, y + 8), slice(x, x + 128)) for y in range(0, rows, 8) for x in range(0, cols, 128)]
 
 
-def peak_kernel(vel, peak):
-    planes, rows, cols = vel.shape[1:]
+def peak_kernel(vel, peak, held, sems):
+    planes, rows, cols = held.shape[1:]
+    count = sems.shape[0]
+    share = planes // count
+    copies = []
+    for part in range(count):
+        span = (slice(None), pl.ds(part * share, share))
+        copies.append(pltpu.make_async_copy(vel.at[span], held.at[span], sems.at[part]))
+        copies[-1].start()
     total = None
-    for at in columns(rows, cols):
-        for k in range(planes):
-            speed = sum(jnp.abs(vel[(comp, k) + at]) for comp in range(3))
-            total = speed if total is None else jnp.maximum(total, speed)
+    for part in range(count):
+        copies[part].wait()
+        for k in range(part * share, (part + 1) * share):
+            for at in columns(rows, cols):
+                speed = sum(jnp.abs(held[(comp, k) + at]) for comp in range(3))
+                total = speed if total is None else jnp.maximum(total, speed)
     peak[...] = jnp.broadcast_to(jnp.max(total, axis=0, keepdims=True), peak.shape)
 
 
@@ -100,9 +109,23 @@
                 out[(comp, k) + at] = (forward[k] - (q1 + q2)) + near
 
 
-def scale_kernel(tendency, peaks, out):
+def scale_kernel(tendency, peaks, out, staged, sems):
+    planes, rows, cols = tendency.shape[1:]
+    count = sems.shape[0]
+    share = planes // count
     scale = COURANT / (jnp.max(peaks[...], keepdims=True) + 1e-06)
-    out[...] = tendency[...] * jnp.broadcast_to(scale.reshape(1, 1, 1, 1), tendency.shape)
+    scale = jnp.broadcast_to(scale, (8, 128))
+    copies = []
+    for part in range(count):
+        for k in range(part * share, (part + 1) * share):
+            for comp in range(3):
+                for at in columns(rows, cols):
+                    staged[(comp, k) + at] = scale * tendency[(comp, k) + at]
+        span = (slice(None), pl.ds(part * share, share))
+        copies.append(pltpu.make_async_copy(staged.at[span], out.at[span], sems.at[part]))
+        copies[-1].start()
+    for copy in copies:
+        copy.wait()
 
 
 def mesh_groups(shape, free):
@@ -145,47 +168,56 @@
         _, planes, rows, cols = velocity.shape
         n_across, n_along = len(across[0]), len(along[0])
         local = pl.BlockSpec(memory_space=pltpu.VMEM)
-        held = in_vmem(velocity)
         packet = pltpu.VMEM((9, rows, cols), jnp.float32)
-        peak = pl.pallas_call(
+        peak, held = pl.pallas_call(
             peak_kernel,
-            out_shape=pltpu.VMEM((n_across, 128), jnp.float32),
-            in_specs=[local],
-            out_specs=local,
+            out_shape=(
+                pltpu.VMEM((n_along, 128), jnp.float32),
+                pltpu.VMEM(velocity.shape, jnp.float32),
+            ),
+            in_specs=[pl.BlockSpec(memory_space=pl.ANY)],
+            out_specs=(local, local),
+            scratch_shapes=[pltpu.SemaphoreType.DMA((8,))],
             cost_estimate=work(0.3),
             name="peak",
-        )(held)
+        )(velocity)
+        held = in_vmem(held)
         rightward, leftward = pl.pallas_call(
             edges_kernel,
             out_shape=(packet, packet),
             in_specs=[local],
             out_specs=(local, local),
-            cost_estimate=work(5),
+            cost_estimate=work(1.0),
             name="edges",
         )(held)
         from_left = in_vmem(lax.ppermute(rightward, "gz", [(i, (i + 1) % slabs) for i in range(slabs)]))
         from_right = in_vmem(lax.ppermute(leftward, "gz", [(i, (i - 1) % slabs) for i in range(slabs)]))
         merged = pl.pallas_call(
             merge_kernel,
-            out_shape=pltpu.VMEM((n_along, 128), jnp.float32),
+            out_shape=pltpu.VMEM((n_across, 128), jnp.float32),
             in_specs=[local],
             out_specs=local,
-            cost_estimate=work(1),
+            cost_estimate=work(100.0),
             name="merge",
-        )(in_vmem(spread(peak, axes, across)))
-        peaks = in_vmem(spread(in_vmem(merged), axes, along))
+        )(in_vmem(spread(peak, axes, along)))
+        peaks = in_vmem(spread(in_vmem(merged), axes, across))
         tendency = pl.pallas_call(
             tendency_kernel,
             out_shape=pltpu.VMEM(velocity.shape, jnp.float32),
             in_specs=[local] * 4,
             out_specs=local,
-            cost_estimate=work(1),
+            cost_estimate=work(1.0),
             name="tendency",
         )(held, from_left, from_right, in_vmem(merged))
         return pl.pallas_call(
             scale_kernel,
             out_shape=jax.ShapeDtypeStruct(velocity.shape, jnp.float32),
             in_specs=[local, local],
+            out_specs=pl.BlockSpec(memory_space=pl.ANY),
+            scratch_shapes=[
+                pltpu.VMEM(velocity.shape, jnp.float32),
+                pltpu.SemaphoreType.DMA((8,)),
+            ],
             name="scale",
         )(in_vmem(tendency), peaks)
 

time: 54.4 us -> 56.1 us (1.031)
  starting transfers between devices: 34.5 us -> 38 us
  waiting for transfers between devices: 14.4 us -> 12.3 us
  Pallas kernels: 4.01 us -> 5.29 us
  local copies, waits for them, and re-layouts: 1.14 us -> 0 us
    ppermute x1, starting transfers between devices: 1.92 us -> 4.39 us  [body(): lax.ppermute(rightward, 'gz', [(i, (i + 1) % slabs) for i in range(slabs)])]
    all_to_all x2, waiting for transfers between devices: 14.4 us -> 12.3 us  [spread(): lax.all_to_all(rows, axes, 0, 0, tiled=True, axis_index_groups=groups)]
    all_to_all x2, starting transfers between devices: 30.1 us -> 31.7 us  [spread(): lax.all_to_all(rows, axes, 0, 0, tiled=True, axis_index_groups=groups)]
    pallas_call x2, Pallas kernels: 1.31 us -> 2.52 us  [the longest x1 1.9 us: body(): pl.pallas_call(peak_kernel, out_shape=(pltpu.VMEM((n_along, 128), jnp.flo...]
    unnamed x4 -> x0, local copies, waits for them, and re-layouts: 1.14 us -> none
where the time goes in v4:
time: 56.1 us; the launch traced here: 55.7 us
  starting transfers between devices  38 us (68%)
  waiting for transfers between devices  12.3 us (22%)
  Pallas kernels  5.29 us (9%)
    all_to_all x2, starting transfers between devices, spread(): lax.all_to_all(rows, axes, 0, 0, tiled=True, axis_index_groups=groups)  31.7 us
    all_to_all x2, waiting for transfers between devices, spread(): lax.all_to_all(rows, axes, 0, 0, tiled=True, axis_index_groups=groups)  12.3 us
    ppermute x1, starting transfers between devices, body(): lax.ppermute(rightward, 'gz', [(i, (i + 1) % slabs) for i in range(slabs)])  4.39 us
    ppermute x1, starting transfers between devices, body(): lax.ppermute(leftward, 'gz', [(i, (i - 1) % slabs) for i in range(slabs)])  1.92 us
    pallas_call x1, Pallas kernels, body(): pl.pallas_call(peak_kernel, out_shape=(pltpu.VMEM((n_along, 128), jnp.flo...  1.9 us
    pallas_call x1, Pallas kernels, body(): pl.pallas_call(tendency_kernel, out_shape=pltpu.VMEM(velocity.shape, jnp....  1.41 us
  transfers between devices with their start and end apart: 4, of which 2 were waited for; matrix products, arithmetic and copies ran while one was open for 0% of the time, Pallas kernels for 4%

profile of v4, /device:TPU:1, one launch (start us, length us, event | category | flops | bytes accessed | tf_op | source)
XLA Modules:
  0.0 55.7 jit_solution(16995120778806608641)
XLA Ops:
  0.0 1.9 %peak.1 = (f32[16,128]{1,0:T(8,128)}, f32[3,16,16,256]{3,2,1,0:T(8,128)S(1)}) custom-call(f32[3,16,16,256]{3,2,1,0:T(8,128)} %vel.1), custom_call_target="tpu_custom_call" | custom-call | flops 300000000 | bytes 900000 | tf_op jit(solution)/shard_map/peak/pallas_call | solution.py:172
  1.9 19.4 %all-to-all-start = ((f32[16,1,128]{2,1,0:T(1,128)}), f32[16,1,128]{2,1,0:T(1,128)S(1)}, u32[]{:S(2)}, u32[]{:S(2)}) async-start(f32[16,1,128]{2,1,0:T(1,128)} %bitcast.1), calls=%async_computation | async-start | bytes 16384 | tf_op jit(solution)/shard_map/all_to_all | solution.py:148
  21.3 0.3 edges.1
  21.6 4.4 %collective-permute-start = (f32[9,16,256]{2,1,0:T(8,128)S(1)}, f32[9,16,256]{2,1,0:T(8,128)S(1)}, u32[]{:S(2)}, u32[]{:S(2)}) collective-permute-start(f32[9,16,256]{2,1,0:T(8,128)S(1)} %get-tuple-element.10), channel_id=1, source_target_pairs={{0,8},{8,16},{16,24},{24,32},{32,40},{40,48},{48,56},{56,64},{64,7... | collective-permute-start | bytes 442376 | tf_op jit(solution)/shard_map/ppermute | solution.py:193
  26.0 1.9 %collective-permute-start.1 = (f32[9,16,256]{2,1,0:T(8,128)S(1)}, f32[9,16,256]{2,1,0:T(8,128)S(1)}, u32[]{:S(2)}, u32[]{:S(2)}) collective-permute-start(f32[9,16,256]{2,1,0:T(8,128)S(1)} %get-tuple-element.11), channel_id=1, source_target_pairs={{0,1016},{8,0},{16,8},{24,16},{32,24},{40,32},{48,40},{56,48},{64,... | collective-permute-start | bytes 442376 | tf_op jit(solution)/shard_map/ppermute | solution.py:194
  28.0 4.6 %all-to-all-done = f32[16,1,128]{2,1,0:T(1,128)S(1)} async-done(((f32[16,1,128]{2,1,0:T(1,128)}), f32[16,1,128]{2,1,0:T(1,128)S(1)}, u32[]{:S(2)}, u32[]{:S(2)}) %all-to-all-start) | async-done | bytes 8224 | tf_op jit(solution)/shard_map/all_to_all | solution.py:148
  32.6 0.6 %merge.1._ = f32[64,128]{1,0:T(8,128)} custom-call(f32[16,128]{1,0:T(8,128)S(1)} %bitcast.9), custom_call_target="tpu_custom_call" | custom-call | flops 99999997952 | bytes 300000000 | tf_op jit(solution)/shard_map/merge/pallas_call | solution.py:195
  33.2 12.3 %all-to-all-start.1 = ((f32[64,1,128]{2,1,0:T(1,128)}), f32[64,1,128]{2,1,0:T(1,128)S(1)}, u32[]{:S(2)}, u32[]{:S(2)}) async-start(f32[64,1,128]{2,1,0:T(1,128)} %bitcast.4), calls=%async_computation.1 | async-start | bytes 65536 | tf_op jit(solution)/shard_map/all_to_all | solution.py:148
  45.5 0.0 collective-permute-done.from_left
  45.5 0.0 collective-permute-done.1.from_right
  45.5 1.4 %tendency.1 = f32[3,16,16,256]{3,2,1,0:T(8,128)S(1)} custom-call(f32[3,16,16,256]{3,2,1,0:T(8,128)S(1)} %get-tuple-element.9.vel, f32[9,16,256]{2,1,0:T(8,128)S(1)} %collective-permute-done.from_left, f32[9,16,256]{2,1,0:T(8,128)S(1)} %collective-permute-done.1.from_right, f32[64,128]{1,0:T(8,128)} %merge.1._), custom_call_target="tpu_custom_call" | custom-call | flops 1000000000 | bytes 3000000 | tf_op jit(solution)/shard_map/tendency/pallas_call | solution.py:204
  46.9 7.7 %all-to-all-done.1 = f32[64,1,128]{2,1,0:T(1,128)S(1)} async-done(((f32[64,1,128]{2,1,0:T(1,128)}), f32[64,1,128]{2,1,0:T(1,128)S(1)}, u32[]{:S(2)}, u32[]{:S(2)}) %all-to-all-start.1) | async-done | bytes 32800 | tf_op jit(solution)/shard_map/all_to_all | solution.py:148
  54.6 1.1 %scale.1 = f32[3,16,16,256]{3,2,1,0:T(8,128)} custom-call(f32[3,16,16,256]{3,2,1,0:T(8,128)S(1)} %tendency.1, f32[64,128]{1,0:T(8,128)S(1)} %bitcast.8), custom_call_target="tpu_custom_call" | custom-call | tf_op jit(solution)/shard_map/scale/pallas_call | solution.py:212
Async XLA Ops:
  1.9 30.7 %all-to-all-start = ((f32[16,1,128]{2,1,0:T(1,128)}), f32[16,1,128]{2,1,0:T(1,128)S(1)}, u32[]{:S(2)}, u32[]{:S(2)}) async-start(f32[16,1,128]{2,1,0:T(1,128)} %bitcast.1), calls=%async_computation | async-start | bytes 16384 | tf_op jit(solution)/shard_map/all_to_all | solution.py:148
  21.6 23.9 %collective-permute-start = (f32[9,16,256]{2,1,0:T(8,128)S(1)}, f32[9,16,256]{2,1,0:T(8,128)S(1)}, u32[]{:S(2)}, u32[]{:S(2)}) collective-permute-start(f32[9,16,256]{2,1,0:T(8,128)S(1)} %get-tuple-element.10), channel_id=1, source_target_pairs={{0,8},{8,16},{16,24},{24,32},{32,40},{40,48},{48,56},{56,64},{64,7... | collective-permute-start | bytes 442376 | tf_op jit(solution)/shard_map/ppermute | solution.py:193
  26.0 19.5 %collective-permute-start.1 = (f32[9,16,256]{2,1,0:T(8,128)S(1)}, f32[9,16,256]{2,1,0:T(8,128)S(1)}, u32[]{:S(2)}, u32[]{:S(2)}) collective-permute-start(f32[9,16,256]{2,1,0:T(8,128)S(1)} %get-tuple-element.11), channel_id=1, source_target_pairs={{0,1016},{8,0},{16,8},{24,16},{32,24},{40,32},{48,40},{56,48},{64,... | collective-permute-start | bytes 442376 | tf_op jit(solution)/shard_map/ppermute | solution.py:194
  33.2 21.4 %all-to-all-start.1 = ((f32[64,1,128]{2,1,0:T(1,128)}), f32[64,1,128]{2,1,0:T(1,128)S(1)}, u32[]{:S(2)}, u32[]{:S(2)}) async-start(f32[64,1,128]{2,1,0:T(1,128)} %bitcast.4), calls=%async_computation.1 | async-start | bytes 65536 | tf_op jit(solution)/shard_map/all_to_all | solution.py:148

commit v5 on v4

--- a/solution.py
+++ b/solution.py
@@ -77,53 +77,45 @@
             leftward[(6 + comp,) + at] = u[0]
 
 
-def tendency_kernel(vel, from_left, from_right, _, out):
+def step_kernel(peaks, step):
+    highest = jnp.max(peaks[...], keepdims=True)
+    step[...] = jnp.broadcast_to(COURANT / (highest + 1e-06), step.shape)
+
+
+def increment_kernel(vel, from_left, from_right, step, out, staged, sems):
     planes, rows, cols = vel.shape[1:]
-    for at in columns(rows, cols):
-        w = [vel[(2, k) + at] for k in range(planes)]
-        w = [from_left[(8,) + at]] + w + [from_right[(8,) + at]]
-        w1 = [A1 * v for v in w]
+    gain1 = A1 * step[...]
+    gain2 = A2 * step[...]
+    copies = []
+    for y in range(0, rows, 8):
         for comp in range(3):
-            if comp == 2:
-                u = w
-            else:
+            for x in range(0, cols, 128):
+                at = (slice(y, y + 8), slice(x, x + 128))
+                w = [vel[(2, k) + at] for k in range(planes)]
+                w = [from_left[(8,) + at]] + w + [from_right[(8,) + at]]
                 u = [vel[(comp, k) + at] for k in range(planes)]
                 u = [from_left[(6 + comp,) + at]] + u + [from_right[(6 + comp,) + at]]
-            f1 = [a * b for a, b in zip(w1, u)]
-            f2 = [A2 * v for v in u]
-            g1 = [f1[k + 1] - f1[k] for k in range(planes + 1)]
-            g2 = [f2[k + 1] - f2[k] for k in range(planes + 1)]
-            p1 = A1 * from_left[(comp,) + at]
-            p2 = A2 * from_left[(3 + comp,) + at]
-            forward = []
-            for k in range(planes):
-                p1 = g1[k] + R1 * p1
-                p2 = g2[k] + R2 * p2
-                forward.append(p2 - p1)
-            q1 = A1 * from_right[(comp,) + at]
-            q2 = A2 * from_right[(3 + comp,) + at]
-            for k in reversed(range(planes)):
-                q1 = g1[k + 1] + R1 * q1
-                q2 = g2[k + 1] + R2 * q2
-                near = (E1 / A1) * (g1[k] + g1[k + 1]) - (E2 / A2) * (g2[k] - g2[k + 1])
-                out[(comp, k) + at] = (forward[k] - (q1 + q2)) + near
-
-
-def scale_kernel(tendency, peaks, out, staged, sems):
-    planes, rows, cols = tendency.shape[1:]
-    count = sems.shape[0]
-    share = planes // count
-    scale = COURANT / (jnp.max(peaks[...], keepdims=True) + 1e-06)
-    scale = jnp.broadcast_to(scale, (8, 128))
-    copies = []
-    for part in range(count):
-        for k in range(part * share, (part + 1) * share):
-            for comp in range(3):
-                for at in columns(rows, cols):
-                    staged[(comp, k) + at] = scale * tendency[(comp, k) + at]
-        span = (slice(None), pl.ds(part * share, share))
-        copies.append(pltpu.make_async_copy(staged.at[span], out.at[span], sems.at[part]))
-        copies[-1].start()
+                f1 = [gain1 * (a * b) for a, b in zip(w, u)]
+                f2 = [gain2 * v for v in u]
+                g1 = [f1[k + 1] - f1[k] for k in range(planes + 1)]
+                g2 = [f2[k + 1] - f2[k] for k in range(planes + 1)]
+                p1 = gain1 * from_left[(comp,) + at]
+                p2 = gain2 * from_left[(3 + comp,) + at]
+                forward = []
+                for k in range(planes):
+                    p1 = g1[k] + R1 * p1
+                    p2 = g2[k] + R2 * p2
+                    forward.append(p2 - p1)
+                q1 = gain1 * from_right[(comp,) + at]
+                q2 = gain2 * from_right[(3 + comp,) + at]
+                for k in reversed(range(planes)):
+                    q1 = g1[k + 1] + R1 * q1
+                    q2 = g2[k + 1] + R2 * q2
+                    near = (E1 / A1) * (g1[k] + g1[k + 1]) - (E2 / A2) * (g2[k] - g2[k + 1])
+                    staged[(comp, k) + at] = (forward[k] - (q1 + q2)) + near
+            span = (comp, slice(None), pl.ds(y, 8))
+            copies.append(pltpu.make_async_copy(staged.at[span], out.at[span], sems.at[len(copies)]))
+            copies[-1].start()
     for copy in copies:
         copy.wait()
 
@@ -161,8 +153,8 @@
     slabs, lines = mesh.shape["gz"], mesh.shape["gy"]
     ring = 16
     shape = (slabs // (2 * ring), ring, 2, lines)
-    across = mesh_groups(shape, (0, 2, 3))
-    along = mesh_groups(shape, (1,))
+    across = mesh_groups(shape, (0, 3))
+    along = mesh_groups(shape, (1, 2))
 
     def body(velocity):
         _, planes, rows, cols = velocity.shape
@@ -199,27 +191,28 @@
             out_specs=local,
             cost_estimate=work(100.0),
             name="merge",
-        )(in_vmem(spread(peak, axes, along)))
-        peaks = in_vmem(spread(in_vmem(merged), axes, across))
-        tendency = pl.pallas_call(
-            tendency_kernel,
-            out_shape=pltpu.VMEM(velocity.shape, jnp.float32),
+        )(in_vmem(spread(in_vmem(peak), axes, along)))
+        merged = in_vmem(merged)
+        peaks = in_vmem(spread(merged, axes, across))
+        step = pl.pallas_call(
+            step_kernel,
+            out_shape=pltpu.VMEM((8, 128), jnp.float32),
+            in_specs=[local],
+            out_specs=local,
+            cost_estimate=work(0.1),
+            name="step",
+        )(peaks)
+        return pl.pallas_call(
+            increment_kernel,
+            out_shape=jax.ShapeDtypeStruct(velocity.shape, jnp.float32),
             in_specs=[local] * 4,
-            out_specs=local,
-            cost_estimate=work(1.0),
-            name="tendency",
-        )(held, from_left, from_right, in_vmem(merged))
-        return pl.pallas_call(
-            scale_kernel,
-            out_shape=jax.ShapeDtypeStruct(velocity.shape, jnp.float32),
-            in_specs=[local, local],
             out_specs=pl.BlockSpec(memory_space=pl.ANY),
             scratch_shapes=[
                 pltpu.VMEM(velocity.shape, jnp.float32),
-                pltpu.SemaphoreType.DMA((8,)),
+                pltpu.SemaphoreType.DMA((3 * rows // 8,)),
             ],
-            name="scale",
-        )(in_vmem(tendency), peaks)
+            name="increment",
+        )(held, from_left, from_right, in_vmem(step))
 
     return jax.shard_map(
         body,

time: 56.1 us -> 54 us (0.963)
  blocking collectives: 0 us -> 18.1 us
  starting transfers between devices: 38 us -> 25.9 us
  waiting for transfers between devices: 12.3 us -> 5.94 us
  Pallas kernels: 5.29 us -> 3.74 us
    all_to_all x0 -> x1, blocking collectives: none -> 18.1 us  [spread(): lax.all_to_all(rows, axes, 0, 0, tiled=True, axis_index_groups=groups)]
    all_to_all x2 -> x1, starting transfers between devices: 31.7 us -> 20.4 us  [spread(): lax.all_to_all(rows, axes, 0, 0, tiled=True, axis_index_groups=groups)]
    all_to_all x2 -> x1, waiting for transfers between devices: 12.3 us -> 5.94 us  [spread(): lax.all_to_all(rows, axes, 0, 0, tiled=True, axis_index_groups=groups)]
    pallas_call x2, Pallas kernels: 2.48 us -> 1.53 us  [the longest x1 1.4 us: body(): pl.pallas_call(increment_kernel, out_shape=jax.ShapeDtypeStruct(velocity....]
    ppermute x1, starting transfers between devices: 4.39 us -> 3.54 us  [body(): lax.ppermute(rightward, 'gz', [(i, (i + 1) % slabs) for i in range(slabs)])]
    pallas_call x1, Pallas kernels: 0.62 us -> 0.01 us  [body(): pl.pallas_call(merge_kernel, out_shape=pltpu.VMEM((n_across, 128), jnp.fl...]
  transfers between devices with their start and end apart: 4 -> 3, of which waited for: 2 -> 1; matrix products, arithmetic and copies ran while one was open for 0% -> 0% of each run, Pallas kernels for 4% -> 1%
where the time goes in v5:
time: 54 us; the launch traced here: 53.7 us
  starting transfers between devices  25.9 us (48%)
  blocking collectives  18.1 us (34%)
  waiting for transfers between devices  5.94 us (11%)
  Pallas kernels  3.74 us (7%)
    all_to_all x1, starting transfers between devices, spread(): lax.all_to_all(rows, axes, 0, 0, tiled=True, axis_index_groups=groups)  20.4 us
    all_to_all x1, blocking collectives, spread(): lax.all_to_all(rows, axes, 0, 0, tiled=True, axis_index_groups=groups)  18.1 us
    all_to_all x1, waiting for transfers between devices, spread(): lax.all_to_all(rows, axes, 0, 0, tiled=True, axis_index_groups=groups)  5.94 us
    ppermute x1, starting transfers between devices, body(): lax.ppermute(rightward, 'gz', [(i, (i + 1) % slabs) for i in range(slabs)])  3.54 us
    ppermute x1, starting transfers between devices, body(): lax.ppermute(leftward, 'gz', [(i, (i - 1) % slabs) for i in range(slabs)])  1.92 us
    pallas_call x1, Pallas kernels, body(): pl.pallas_call(peak_kernel, out_shape=(pltpu.VMEM((n_along, 128), jnp.flo...  1.91 us
    pallas_call x1, Pallas kernels, body(): pl.pallas_call(increment_kernel, out_shape=jax.ShapeDtypeStruct(velocity....  1.4 us
  transfers between devices with their start and end apart: 3, of which 1 were waited for; matrix products, arithmetic and copies ran while one was open for 0% of the time, Pallas kernels for 1%

profile of v5, /device:TPU:1, one launch (start us, length us, event | category | flops | bytes accessed | tf_op | source)
XLA Modules:
  0.0 53.7 jit_solution(13737813856197982786)
XLA Ops:
  0.0 1.9 %peak.1 = (f32[32,128]{1,0:T(8,128)}, f32[3,16,16,256]{3,2,1,0:T(8,128)S(1)}) custom-call(f32[3,16,16,256]{3,2,1,0:T(8,128)} %vel.1), custom_call_target="tpu_custom_call" | custom-call | flops 300000000 | bytes 900000 | tf_op jit(solution)/shard_map/peak/pallas_call | solution.py:164
  1.9 20.4 %all-to-all-start = ((f32[32,1,128]{2,1,0:T(1,128)}), f32[32,1,128]{2,1,0:T(1,128)S(1)}, u32[]{:S(2)}, u32[]{:S(2)}) async-start(f32[32,1,128]{2,1,0:T(1,128)} %bitcast.1), calls=%async_computation | async-start | bytes 32768 | tf_op jit(solution)/shard_map/all_to_all | solution.py:140
  22.4 0.3 edges.1
  22.7 3.5 %collective-permute-start = (f32[9,16,256]{2,1,0:T(8,128)S(1)}, f32[9,16,256]{2,1,0:T(8,128)S(1)}, u32[]{:S(2)}, u32[]{:S(2)}) collective-permute-start(f32[9,16,256]{2,1,0:T(8,128)S(1)} %get-tuple-element.10), channel_id=1, source_target_pairs={{0,8},{8,16},{16,24},{24,32},{32,40},{40,48},{48,56},{56,64},{64,7... | collective-permute-start | bytes 442376 | tf_op jit(solution)/shard_map/ppermute | solution.py:185
  26.2 1.9 %collective-permute-start.1 = (f32[9,16,256]{2,1,0:T(8,128)S(1)}, f32[9,16,256]{2,1,0:T(8,128)S(1)}, u32[]{:S(2)}, u32[]{:S(2)}) collective-permute-start(f32[9,16,256]{2,1,0:T(8,128)S(1)} %get-tuple-element.11), channel_id=1, source_target_pairs={{0,1016},{8,0},{16,8},{24,16},{32,24},{40,32},{48,40},{56,48},{64,... | collective-permute-start | bytes 442376 | tf_op jit(solution)/shard_map/ppermute | solution.py:186
  28.1 5.9 %all-to-all-done = f32[32,1,128]{2,1,0:T(1,128)S(1)} async-done(((f32[32,1,128]{2,1,0:T(1,128)}), f32[32,1,128]{2,1,0:T(1,128)S(1)}, u32[]{:S(2)}, u32[]{:S(2)}) %all-to-all-start) | async-done | bytes 16416 | tf_op jit(solution)/shard_map/all_to_all | solution.py:140
  34.1 18.1 %all_to_all.22 = f32[32,1,128]{2,1,0:T(1,128)S(1)} all-to-all(f32[32,1,128]{2,1,0:T(1,128)S(1)} %bitcast.9), channel_id=1, replica_groups={{0,1,2,3,4,5,6,7,256,257,258,259,260,261,262,263,512,513,514,515,516,51..., dimensions={0} | all-to-all | bytes 32768 | tf_op jit(solution)/shard_map/all_to_all | solution.py:140
  52.2 0.1 step.1
  52.3 0.0 collective-permute-done.from_left
  52.3 0.0 collective-permute-done.1.from_right
  52.3 1.4 %increment.1 = f32[3,16,16,256]{3,2,1,0:T(8,128)} custom-call(f32[3,16,16,256]{3,2,1,0:T(8,128)S(1)} %get-tuple-element.9.vel, f32[9,16,256]{2,1,0:T(8,128)S(1)} %collective-permute-done.from_left, f32[9,16,256]{2,1,0:T(8,128)S(1)} %collective-permute-done.1.from_right, f32[8,128]{1,0:T(8,128)S(1)} %step.1), custom_call_target="tpu_custom_call" | custom-call | tf_op jit(solution)/shard_map/increment/pallas_call | solution.py:205
  (1 shorter events, 0.0 us)
Async XLA Ops:
  1.9 32.2 %all-to-all-start = ((f32[32,1,128]{2,1,0:T(1,128)}), f32[32,1,128]{2,1,0:T(1,128)S(1)}, u32[]{:S(2)}, u32[]{:S(2)}) async-start(f32[32,1,128]{2,1,0:T(1,128)} %bitcast.1), calls=%async_computation | async-start | bytes 32768 | tf_op jit(solution)/shard_map/all_to_all | solution.py:140
  22.7 29.7 %collective-permute-start = (f32[9,16,256]{2,1,0:T(8,128)S(1)}, f32[9,16,256]{2,1,0:T(8,128)S(1)}, u32[]{:S(2)}, u32[]{:S(2)}) collective-permute-start(f32[9,16,256]{2,1,0:T(8,128)S(1)} %get-tuple-element.10), channel_id=1, source_target_pairs={{0,8},{8,16},{16,24},{24,32},{32,40},{40,48},{48,56},{56,64},{64,7... | collective-permute-start | bytes 442376 | tf_op jit(solution)/shard_map/ppermute | solution.py:185
  26.2 26.1 %collective-permute-start.1 = (f32[9,16,256]{2,1,0:T(8,128)S(1)}, f32[9,16,256]{2,1,0:T(8,128)S(1)}, u32[]{:S(2)}, u32[]{:S(2)}) collective-permute-start(f32[9,16,256]{2,1,0:T(8,128)S(1)} %get-tuple-element.11), channel_id=1, source_target_pairs={{0,1016},{8,0},{16,8},{24,16},{32,24},{40,32},{48,40},{56,48},{64,... | collective-permute-start | bytes 442376 | tf_op jit(solution)/shard_map/ppermute | solution.py:186

commit v6 on v5

--- a/solution.py
+++ b/solution.py
@@ -153,8 +153,8 @@
     slabs, lines = mesh.shape["gz"], mesh.shape["gy"]
     ring = 16
     shape = (slabs // (2 * ring), ring, 2, lines)
-    across = mesh_groups(shape, (0, 3))
-    along = mesh_groups(shape, (1, 2))
+    across = [g[::-1] for g in mesh_groups(shape, (0, 3))]
+    along = [g[::-1] for g in mesh_groups(shape, (1, 2))]
 
     def body(velocity):
         _, planes, rows, cols = velocity.shape

time: 54 us -> 48.8 us (0.904)
  blocking collectives: 18.1 us -> 15 us
  waiting for transfers between devices: 5.94 us -> 3.86 us
    all_to_all x1, blocking collectives: 18.1 us -> 15 us  [spread(): lax.all_to_all(rows, axes, 0, 0, tiled=True, axis_index_groups=groups)]
    all_to_all x1, waiting for transfers between devices: 5.94 us -> 3.85 us  [spread(): lax.all_to_all(rows, axes, 0, 0, tiled=True, axis_index_groups=groups)]
where the time goes in v6:
time: 48.8 us; the launch traced here: 48.6 us
  starting transfers between devices  25.9 us (53%)
  blocking collectives  15 us (31%)
  waiting for transfers between devices  3.86 us (8%)
  Pallas kernels  3.74 us (8%)
    all_to_all x1, starting transfers between devices, spread(): lax.all_to_all(rows, axes, 0, 0, tiled=True, axis_index_groups=groups)  20.6 us
    all_to_all x1, blocking collectives, spread(): lax.all_to_all(rows, axes, 0, 0, tiled=True, axis_index_groups=groups)  15 us
    all_to_all x1, waiting for transfers between devices, spread(): lax.all_to_all(rows, axes, 0, 0, tiled=True, axis_index_groups=groups)  3.85 us
    ppermute x1, starting transfers between devices, body(): lax.ppermute(rightward, 'gz', [(i, (i + 1) % slabs) for i in range(slabs)])  3.39 us
    ppermute x1, starting transfers between devices, body(): lax.ppermute(leftward, 'gz', [(i, (i - 1) % slabs) for i in range(slabs)])  1.92 us
    pallas_call x1, Pallas kernels, body(): pl.pallas_call(peak_kernel, out_shape=(pltpu.VMEM((n_along, 128), jnp.flo...  1.91 us
    pallas_call x1, Pallas kernels, body(): pl.pallas_call(increment_kernel, out_shape=jax.ShapeDtypeStruct(velocity....  1.4 us
  transfers between devices with their start and end apart: 3, of which 1 were waited for; matrix products, arithmetic and copies ran while one was open for 0% of the time, Pallas kernels for 1%

profile of v6, /device:TPU:1, one launch (start us, length us, event | category | flops | bytes accessed | tf_op | source)
XLA Modules:
  0.0 48.6 jit_solution(2717132357877564101)
XLA Ops:
  0.0 1.9 %peak.1 = (f32[32,128]{1,0:T(8,128)}, f32[3,16,16,256]{3,2,1,0:T(8,128)S(1)}) custom-call(f32[3,16,16,256]{3,2,1,0:T(8,128)} %vel.1), custom_call_target="tpu_custom_call" | custom-call | flops 300000000 | bytes 900000 | tf_op jit(solution)/shard_map/peak/pallas_call | solution.py:164
  1.9 20.6 %all-to-all-start = ((f32[32,1,128]{2,1,0:T(1,128)}), f32[32,1,128]{2,1,0:T(1,128)S(1)}, u32[]{:S(2)}, u32[]{:S(2)}) async-start(f32[32,1,128]{2,1,0:T(1,128)} %bitcast.1), calls=%async_computation | async-start | bytes 32768 | tf_op jit(solution)/shard_map/all_to_all | solution.py:140
  22.5 0.3 edges.1
  22.8 3.4 %collective-permute-start = (f32[9,16,256]{2,1,0:T(8,128)S(1)}, f32[9,16,256]{2,1,0:T(8,128)S(1)}, u32[]{:S(2)}, u32[]{:S(2)}) collective-permute-start(f32[9,16,256]{2,1,0:T(8,128)S(1)} %get-tuple-element.10), channel_id=1, source_target_pairs={{0,8},{8,16},{16,24},{24,32},{32,40},{40,48},{48,56},{56,64},{64,7... | collective-permute-start | bytes 442376 | tf_op jit(solution)/shard_map/ppermute | solution.py:185
  26.2 1.9 %collective-permute-start.1 = (f32[9,16,256]{2,1,0:T(8,128)S(1)}, f32[9,16,256]{2,1,0:T(8,128)S(1)}, u32[]{:S(2)}, u32[]{:S(2)}) collective-permute-start(f32[9,16,256]{2,1,0:T(8,128)S(1)} %get-tuple-element.11), channel_id=1, source_target_pairs={{0,1016},{8,0},{16,8},{24,16},{32,24},{40,32},{48,40},{56,48},{64,... | collective-permute-start | bytes 442376 | tf_op jit(solution)/shard_map/ppermute | solution.py:186
  28.1 3.9 %all-to-all-done = f32[32,1,128]{2,1,0:T(1,128)S(1)} async-done(((f32[32,1,128]{2,1,0:T(1,128)}), f32[32,1,128]{2,1,0:T(1,128)S(1)}, u32[]{:S(2)}, u32[]{:S(2)}) %all-to-all-start) | async-done | bytes 16416 | tf_op jit(solution)/shard_map/all_to_all | solution.py:140
  32.0 15.0 %all_to_all.22 = f32[32,1,128]{2,1,0:T(1,128)S(1)} all-to-all(f32[32,1,128]{2,1,0:T(1,128)S(1)} %bitcast.9), channel_id=1, replica_groups={{775,774,773,772,771,770,769,768,519,518,517,516,515,514,513,512,263,26..., dimensions={0} | all-to-all | bytes 32768 | tf_op jit(solution)/shard_map/all_to_all | solution.py:140
  47.0 0.1 step.1
  47.1 0.0 collective-permute-done.from_left
  47.1 0.0 collective-permute-done.1.from_right
  47.2 1.4 %increment.1 = f32[3,16,16,256]{3,2,1,0:T(8,128)} custom-call(f32[3,16,16,256]{3,2,1,0:T(8,128)S(1)} %get-tuple-element.9.vel, f32[9,16,256]{2,1,0:T(8,128)S(1)} %collective-permute-done.from_left, f32[9,16,256]{2,1,0:T(8,128)S(1)} %collective-permute-done.1.from_right, f32[8,128]{1,0:T(8,128)S(1)} %step.1), custom_call_target="tpu_custom_call" | custom-call | tf_op jit(solution)/shard_map/increment/pallas_call | solution.py:205
  (1 shorter events, 0.0 us)
Async XLA Ops:
  1.9 30.0 %all-to-all-start = ((f32[32,1,128]{2,1,0:T(1,128)}), f32[32,1,128]{2,1,0:T(1,128)S(1)}, u32[]{:S(2)}, u32[]{:S(2)}) async-start(f32[32,1,128]{2,1,0:T(1,128)} %bitcast.1), calls=%async_computation | async-start | bytes 32768 | tf_op jit(solution)/shard_map/all_to_all | solution.py:140
  22.8 24.4 %collective-permute-start = (f32[9,16,256]{2,1,0:T(8,128)S(1)}, f32[9,16,256]{2,1,0:T(8,128)S(1)}, u32[]{:S(2)}, u32[]{:S(2)}) collective-permute-start(f32[9,16,256]{2,1,0:T(8,128)S(1)} %get-tuple-element.10), channel_id=1, source_target_pairs={{0,8},{8,16},{16,24},{24,32},{32,40},{40,48},{48,56},{56,64},{64,7... | collective-permute-start | bytes 442376 | tf_op jit(solution)/shard_map/ppermute | solution.py:185
  26.2 21.0 %collective-permute-start.1 = (f32[9,16,256]{2,1,0:T(8,128)S(1)}, f32[9,16,256]{2,1,0:T(8,128)S(1)}, u32[]{:S(2)}, u32[]{:S(2)}) collective-permute-start(f32[9,16,256]{2,1,0:T(8,128)S(1)} %get-tuple-element.11), channel_id=1, source_target_pairs={{0,1016},{8,0},{16,8},{24,16},{32,24},{40,32},{48,40},{56,48},{64,... | collective-permute-start | bytes 442376 | tf_op jit(solution)/shard_map/ppermute | solution.py:186

commit v7 on v6

--- a/solution.py
+++ b/solution.py
@@ -136,6 +136,15 @@
     return list(groups.values())
 
 
+def far_first(group, columns, lines):
+    def distance(place):
+        x, y = divmod(place, lines)
+        return min(x, columns - x) + min(y, lines - y)
+
+    places = sorted(range(len(group)), key=lambda place: (distance(place), place), reverse=True)
+    return [group[place] for place in places]
+
+
 def spread(rows, axes, groups):
     return lax.all_to_all(rows, axes, 0, 0, tiled=True, axis_index_groups=groups)
 
@@ -153,8 +162,8 @@
     slabs, lines = mesh.shape["gz"], mesh.shape["gy"]
     ring = 16
     shape = (slabs // (2 * ring), ring, 2, lines)
-    across = [g[::-1] for g in mesh_groups(shape, (0, 3))]
-    along = [g[::-1] for g in mesh_groups(shape, (1, 2))]
+    along = [group[::-1] for group in mesh_groups(shape, (1, 2))]
+    across = [far_first(group, shape[0], lines) for group in mesh_groups(shape, (0, 3))]
 
     def body(velocity):
         _, planes, rows, cols = velocity.shape

time: 48.8 us -> 46.2 us (0.947)
  blocking collectives: 15 us -> 12.2 us
    all_to_all x1, blocking collectives: 15 us -> 12.2 us  [spread(): lax.all_to_all(rows, axes, 0, 0, tiled=True, axis_index_groups=groups)]
where the time goes in v7:
time: 46.2 us; the launch traced here: 45.7 us
  starting transfers between devices  25.9 us (56%)
  blocking collectives  12.2 us (26%)
  waiting for transfers between devices  3.86 us (8%)
  Pallas kernels  3.74 us (8%)
    all_to_all x1, starting transfers between devices, spread(): lax.all_to_all(rows, axes, 0, 0, tiled=True, axis_index_groups=groups)  20.6 us
    all_to_all x1, blocking collectives, spread(): lax.all_to_all(rows, axes, 0, 0, tiled=True, axis_index_groups=groups)  12.2 us
    all_to_all x1, waiting for transfers between devices, spread(): lax.all_to_all(rows, axes, 0, 0, tiled=True, axis_index_groups=groups)  3.85 us
    ppermute x1, starting transfers between devices, body(): lax.ppermute(rightward, 'gz', [(i, (i + 1) % slabs) for i in range(slabs)])  3.39 us
    ppermute x1, starting transfers between devices, body(): lax.ppermute(leftward, 'gz', [(i, (i - 1) % slabs) for i in range(slabs)])  1.92 us
    pallas_call x1, Pallas kernels, body(): pl.pallas_call(peak_kernel, out_shape=(pltpu.VMEM((n_along, 128), jnp.flo...  1.91 us
    pallas_call x1, Pallas kernels, body(): pl.pallas_call(increment_kernel, out_shape=jax.ShapeDtypeStruct(velocity....  1.4 us
  transfers between devices with their start and end apart: 3, of which 1 were waited for; matrix products, arithmetic and copies ran while one was open for 0% of the time, Pallas kernels for 1%

profile of v7, /device:TPU:1, one launch (start us, length us, event | category | flops | bytes accessed | tf_op | source)
XLA Modules:
  0.0 45.7 jit_solution(9964466016526375797)
XLA Ops:
  0.0 1.9 %peak.1 = (f32[32,128]{1,0:T(8,128)}, f32[3,16,16,256]{3,2,1,0:T(8,128)S(1)}) custom-call(f32[3,16,16,256]{3,2,1,0:T(8,128)} %vel.1), custom_call_target="tpu_custom_call" | custom-call | flops 300000000 | bytes 900000 | tf_op jit(solution)/shard_map/peak/pallas_call | solution.py:173
  1.9 20.6 %all-to-all-start = ((f32[32,1,128]{2,1,0:T(1,128)}), f32[32,1,128]{2,1,0:T(1,128)S(1)}, u32[]{:S(2)}, u32[]{:S(2)}) async-start(f32[32,1,128]{2,1,0:T(1,128)} %bitcast.1), calls=%async_computation | async-start | bytes 32768 | tf_op jit(solution)/shard_map/all_to_all | solution.py:149
  22.5 0.3 edges.1
  22.8 3.4 %collective-permute-start = (f32[9,16,256]{2,1,0:T(8,128)S(1)}, f32[9,16,256]{2,1,0:T(8,128)S(1)}, u32[]{:S(2)}, u32[]{:S(2)}) collective-permute-start(f32[9,16,256]{2,1,0:T(8,128)S(1)} %get-tuple-element.10), channel_id=1, source_target_pairs={{0,8},{8,16},{16,24},{24,32},{32,40},{40,48},{48,56},{56,64},{64,7... | collective-permute-start | bytes 442376 | tf_op jit(solution)/shard_map/ppermute | solution.py:194
  26.2 1.9 %collective-permute-start.1 = (f32[9,16,256]{2,1,0:T(8,128)S(1)}, f32[9,16,256]{2,1,0:T(8,128)S(1)}, u32[]{:S(2)}, u32[]{:S(2)}) collective-permute-start(f32[9,16,256]{2,1,0:T(8,128)S(1)} %get-tuple-element.11), channel_id=1, source_target_pairs={{0,1016},{8,0},{16,8},{24,16},{32,24},{40,32},{48,40},{56,48},{64,... | collective-permute-start | bytes 442376 | tf_op jit(solution)/shard_map/ppermute | solution.py:195
  28.1 3.9 %all-to-all-done = f32[32,1,128]{2,1,0:T(1,128)S(1)} async-done(((f32[32,1,128]{2,1,0:T(1,128)}), f32[32,1,128]{2,1,0:T(1,128)S(1)}, u32[]{:S(2)}, u32[]{:S(2)}) %all-to-all-start) | async-done | bytes 16416 | tf_op jit(solution)/shard_map/all_to_all | solution.py:149
  32.0 12.2 %all_to_all.22 = f32[32,1,128]{2,1,0:T(1,128)S(1)} all-to-all(f32[32,1,128]{2,1,0:T(1,128)S(1)} %bitcast.9), channel_id=1, replica_groups={{516,772,517,515,260,773,771,518,514,261,259,4,774,770,519,513,262,258,..., dimensions={0} | all-to-all | bytes 32768 | tf_op jit(solution)/shard_map/all_to_all | solution.py:149
  44.2 0.1 step.1
  44.3 0.0 collective-permute-done.from_left
  44.3 0.0 collective-permute-done.1.from_right
  44.3 1.4 %increment.1 = f32[3,16,16,256]{3,2,1,0:T(8,128)} custom-call(f32[3,16,16,256]{3,2,1,0:T(8,128)S(1)} %get-tuple-element.9.vel, f32[9,16,256]{2,1,0:T(8,128)S(1)} %collective-permute-done.from_left, f32[9,16,256]{2,1,0:T(8,128)S(1)} %collective-permute-done.1.from_right, f32[8,128]{1,0:T(8,128)S(1)} %step.1), custom_call_target="tpu_custom_call" | custom-call | tf_op jit(solution)/shard_map/increment/pallas_call | solution.py:214
  (1 shorter events, 0.0 us)
Async XLA Ops:
  1.9 30.0 %all-to-all-start = ((f32[32,1,128]{2,1,0:T(1,128)}), f32[32,1,128]{2,1,0:T(1,128)S(1)}, u32[]{:S(2)}, u32[]{:S(2)}) async-start(f32[32,1,128]{2,1,0:T(1,128)} %bitcast.1), calls=%async_computation | async-start | bytes 32768 | tf_op jit(solution)/shard_map/all_to_all | solution.py:149
  22.8 21.5 %collective-permute-start = (f32[9,16,256]{2,1,0:T(8,128)S(1)}, f32[9,16,256]{2,1,0:T(8,128)S(1)}, u32[]{:S(2)}, u32[]{:S(2)}) collective-permute-start(f32[9,16,256]{2,1,0:T(8,128)S(1)} %get-tuple-element.10), channel_id=1, source_target_pairs={{0,8},{8,16},{16,24},{24,32},{32,40},{40,48},{48,56},{56,64},{64,7... | collective-permute-start | bytes 442376 | tf_op jit(solution)/shard_map/ppermute | solution.py:194
  26.2 18.2 %collective-permute-start.1 = (f32[9,16,256]{2,1,0:T(8,128)S(1)}, f32[9,16,256]{2,1,0:T(8,128)S(1)}, u32[]{:S(2)}, u32[]{:S(2)}) collective-permute-start(f32[9,16,256]{2,1,0:T(8,128)S(1)} %get-tuple-element.11), channel_id=1, source_target_pairs={{0,1016},{8,0},{16,8},{24,16},{32,24},{40,32},{48,40},{56,48},{64,... | collective-permute-start | bytes 442376 | tf_op jit(solution)/shard_map/ppermute | solution.py:195

commit v8 on v7

--- a/solution.py
+++ b/solution.py
@@ -77,15 +77,11 @@
             leftward[(6 + comp,) + at] = u[0]
 
 
-def step_kernel(peaks, step):
-    highest = jnp.max(peaks[...], keepdims=True)
-    step[...] = jnp.broadcast_to(COURANT / (highest + 1e-06), step.shape)
-
-
-def increment_kernel(vel, from_left, from_right, step, out, staged, sems):
+def increment_kernel(vel, from_left, from_right, peaks, out, staged, sems):
     planes, rows, cols = vel.shape[1:]
-    gain1 = A1 * step[...]
-    gain2 = A2 * step[...]
+    step = jnp.broadcast_to(COURANT / (jnp.max(peaks[...], keepdims=True) + 1e-06), (8, 128))
+    gain1 = A1 * step
+    gain2 = A2 * step
     copies = []
     for y in range(0, rows, 8):
         for comp in range(3):
@@ -203,14 +199,6 @@
         )(in_vmem(spread(in_vmem(peak), axes, along)))
         merged = in_vmem(merged)
         peaks = in_vmem(spread(merged, axes, across))
-        step = pl.pallas_call(
-            step_kernel,
-            out_shape=pltpu.VMEM((8, 128), jnp.float32),
-            in_specs=[local],
-            out_specs=local,
-            cost_estimate=work(0.1),
-            name="step",
-        )(peaks)
         return pl.pallas_call(
             increment_kernel,
             out_shape=jax.ShapeDtypeStruct(velocity.shape, jnp.float32),
@@ -221,7 +209,7 @@
                 pltpu.SemaphoreType.DMA((3 * rows // 8,)),
             ],
             name="increment",
-        )(held, from_left, from_right, in_vmem(step))
+        )(held, from_left, from_right, peaks)
 
     return jax.shard_map(
         body,

time: 46.2 us -> 46.2 us (level)
  no operation moved by 1% of the time
where the time goes in v8:
time: 46.2 us; the launch traced here: 45.6 us
  starting transfers between devices  25.9 us (56%)
  blocking collectives  12.2 us (26%)
  waiting for transfers between devices  3.86 us (8%)
  Pallas kernels  3.67 us (8%)
    all_to_all x1, starting transfers between devices, spread(): lax.all_to_all(rows, axes, 0, 0, tiled=True, axis_index_groups=groups)  20.6 us
    all_to_all x1, blocking collectives, spread(): lax.all_to_all(rows, axes, 0, 0, tiled=True, axis_index_groups=groups)  12.2 us
    all_to_all x1, waiting for transfers between devices, spread(): lax.all_to_all(rows, axes, 0, 0, tiled=True, axis_index_groups=groups)  3.85 us
    ppermute x1, starting transfers between devices, body(): lax.ppermute(rightward, 'gz', [(i, (i + 1) % slabs) for i in range(slabs)])  3.39 us
    ppermute x1, starting transfers between devices, body(): lax.ppermute(leftward, 'gz', [(i, (i - 1) % slabs) for i in range(slabs)])  1.92 us
    pallas_call x1, Pallas kernels, body(): pl.pallas_call(peak_kernel, out_shape=(pltpu.VMEM((n_along, 128), jnp.flo...  1.91 us
    pallas_call x1, Pallas kernels, body(): pl.pallas_call(increment_kernel, out_shape=jax.ShapeDtypeStruct(velocity....  1.45 us
  transfers between devices with their start and end apart: 3, of which 1 were waited for; matrix products, arithmetic and copies ran while one was open for 0% of the time, Pallas kernels for 1%

profile of v8, /device:TPU:1, one launch (start us, length us, event | category | flops | bytes accessed | tf_op | source)
XLA Modules:
  0.0 45.6 jit_solution(8127856732060118026)
XLA Ops:
  0.0 1.9 %peak.1 = (f32[32,128]{1,0:T(8,128)}, f32[3,16,16,256]{3,2,1,0:T(8,128)S(1)}) custom-call(f32[3,16,16,256]{3,2,1,0:T(8,128)} %vel.1), custom_call_target="tpu_custom_call" | custom-call | flops 300000000 | bytes 900000 | tf_op jit(solution)/shard_map/peak/pallas_call | solution.py:169
  1.9 20.6 %all-to-all-start = ((f32[32,1,128]{2,1,0:T(1,128)}), f32[32,1,128]{2,1,0:T(1,128)S(1)}, u32[]{:S(2)}, u32[]{:S(2)}) async-start(f32[32,1,128]{2,1,0:T(1,128)} %bitcast.1), calls=%async_computation | async-start | bytes 32768 | tf_op jit(solution)/shard_map/all_to_all | solution.py:145
  22.5 0.3 edges.1
  22.8 3.4 %collective-permute-start = (f32[9,16,256]{2,1,0:T(8,128)S(1)}, f32[9,16,256]{2,1,0:T(8,128)S(1)}, u32[]{:S(2)}, u32[]{:S(2)}) collective-permute-start(f32[9,16,256]{2,1,0:T(8,128)S(1)} %get-tuple-element.10), channel_id=1, source_target_pairs={{0,8},{8,16},{16,24},{24,32},{32,40},{40,48},{48,56},{56,64},{64,7... | collective-permute-start | bytes 442376 | tf_op jit(solution)/shard_map/ppermute | solution.py:190
  26.2 1.9 %collective-permute-start.1 = (f32[9,16,256]{2,1,0:T(8,128)S(1)}, f32[9,16,256]{2,1,0:T(8,128)S(1)}, u32[]{:S(2)}, u32[]{:S(2)}) collective-permute-start(f32[9,16,256]{2,1,0:T(8,128)S(1)} %get-tuple-element.11), channel_id=1, source_target_pairs={{0,1016},{8,0},{16,8},{24,16},{32,24},{40,32},{48,40},{56,48},{64,... | collective-permute-start | bytes 442376 | tf_op jit(solution)/shard_map/ppermute | solution.py:191
  28.1 3.9 %all-to-all-done = f32[32,1,128]{2,1,0:T(1,128)S(1)} async-done(((f32[32,1,128]{2,1,0:T(1,128)}), f32[32,1,128]{2,1,0:T(1,128)S(1)}, u32[]{:S(2)}, u32[]{:S(2)}) %all-to-all-start) | async-done | bytes 16416 | tf_op jit(solution)/shard_map/all_to_all | solution.py:145
  32.0 12.2 %all_to_all.22 = f32[32,1,128]{2,1,0:T(1,128)S(1)} all-to-all(f32[32,1,128]{2,1,0:T(1,128)S(1)} %bitcast.10), channel_id=1, replica_groups={{516,772,517,515,260,773,771,518,514,261,259,4,774,770,519,513,262,258,..., dimensions={0} | all-to-all | bytes 32768 | tf_op jit(solution)/shard_map/all_to_all | solution.py:145
  44.2 0.0 collective-permute-done.from_left
  44.2 0.0 collective-permute-done.1.from_right
  44.2 1.5 %increment.1 = f32[3,16,16,256]{3,2,1,0:T(8,128)} custom-call(f32[3,16,16,256]{3,2,1,0:T(8,128)S(1)} %get-tuple-element.9.vel, f32[9,16,256]{2,1,0:T(8,128)S(1)} %collective-permute-done.from_left, f32[9,16,256]{2,1,0:T(8,128)S(1)} %collective-permute-done.1.from_right, f32[32,128]{1,0:T(8,128)S(1)} %bitcast.8), custom_call_target="tpu_custom_call" | custom-call | tf_op jit(solution)/shard_map/increment/pallas_call | solution.py:202
  (1 shorter events, 0.0 us)
Async XLA Ops:
  1.9 30.0 %all-to-all-start = ((f32[32,1,128]{2,1,0:T(1,128)}), f32[32,1,128]{2,1,0:T(1,128)S(1)}, u32[]{:S(2)}, u32[]{:S(2)}) async-start(f32[32,1,128]{2,1,0:T(1,128)} %bitcast.1), calls=%async_computation | async-start | bytes 32768 | tf_op jit(solution)/shard_map/all_to_all | solution.py:145
  22.8 21.4 %collective-permute-start = (f32[9,16,256]{2,1,0:T(8,128)S(1)}, f32[9,16,256]{2,1,0:T(8,128)S(1)}, u32[]{:S(2)}, u32[]{:S(2)}) collective-permute-start(f32[9,16,256]{2,1,0:T(8,128)S(1)} %get-tuple-element.10), channel_id=1, source_target_pairs={{0,8},{8,16},{16,24},{24,32},{32,40},{40,48},{48,56},{56,64},{64,7... | collective-permute-start | bytes 442376 | tf_op jit(solution)/shard_map/ppermute | solution.py:190
  26.2 18.0 %collective-permute-start.1 = (f32[9,16,256]{2,1,0:T(8,128)S(1)}, f32[9,16,256]{2,1,0:T(8,128)S(1)}, u32[]{:S(2)}, u32[]{:S(2)}) collective-permute-start(f32[9,16,256]{2,1,0:T(8,128)S(1)} %get-tuple-element.11), channel_id=1, source_target_pairs={{0,1016},{8,0},{16,8},{24,16},{32,24},{40,32},{48,40},{56,48},{64,... | collective-permute-start | bytes 442376 | tf_op jit(solution)/shard_map/ppermute | solution.py:191

commit v9 on v8

--- a/solution.py
+++ b/solution.py
@@ -37,20 +37,18 @@
 
 def peak_kernel(vel, peak, held, sems):
     planes, rows, cols = held.shape[1:]
-    count = sems.shape[0]
-    share = planes // count
-    copies = []
-    for part in range(count):
-        span = (slice(None), pl.ds(part * share, share))
-        copies.append(pltpu.make_async_copy(vel.at[span], held.at[span], sems.at[part]))
-        copies[-1].start()
-    total = None
-    for part in range(count):
-        copies[part].wait()
-        for k in range(part * share, (part + 1) * share):
-            for at in columns(rows, cols):
-                speed = sum(jnp.abs(held[(comp, k) + at]) for comp in range(3))
-                total = speed if total is None else jnp.maximum(total, speed)
+    copy = pltpu.make_async_copy(vel, held, sems.at[0])
+    copy.start()
+    copy.wait()
+    totals = [None] * 8
+    for k in range(planes):
+        for i, at in enumerate(columns(rows, cols)):
+            slot = (k * len(columns(rows, cols)) + i) % len(totals)
+            speed = sum(jnp.abs(held[(comp, k) + at]) for comp in range(3))
+            totals[slot] = speed if totals[slot] is None else jnp.maximum(totals[slot], speed)
+    while len(totals) > 1:
+        totals = [jnp.maximum(a, b) for a, b in zip(totals[::2], totals[1::2])]
+    total = totals[0]
     peak[...] = jnp.broadcast_to(jnp.max(total, axis=0, keepdims=True), peak.shape)
 
 
@@ -174,7 +172,7 @@
             ),
             in_specs=[pl.BlockSpec(memory_space=pl.ANY)],
             out_specs=(local, local),
-            scratch_shapes=[pltpu.SemaphoreType.DMA((8,))],
+            scratch_shapes=[pltpu.SemaphoreType.DMA((1,))],
             cost_estimate=work(0.3),
             name="peak",
         )(velocity)

time: 46.2 us -> 46.1 us (level)
  no operation moved by 1% of the time
where the time goes in v9:
time: 46.1 us; the launch traced here: 45.6 us
  starting transfers between devices  25.9 us (56%)
  blocking collectives  12.2 us (26%)
  waiting for transfers between devices  3.86 us (8%)
  Pallas kernels  3.58 us (8%)
    all_to_all x1, starting transfers between devices, spread(): lax.all_to_all(rows, axes, 0, 0, tiled=True, axis_index_groups=groups)  20.6 us
    all_to_all x1, blocking collectives, spread(): lax.all_to_all(rows, axes, 0, 0, tiled=True, axis_index_groups=groups)  12.2 us
    all_to_all x1, waiting for transfers between devices, spread(): lax.all_to_all(rows, axes, 0, 0, tiled=True, axis_index_groups=groups)  3.85 us
    ppermute x1, starting transfers between devices, body(): lax.ppermute(rightward, 'gz', [(i, (i + 1) % slabs) for i in range(slabs)])  3.39 us
    ppermute x1, starting transfers between devices, body(): lax.ppermute(leftward, 'gz', [(i, (i - 1) % slabs) for i in range(slabs)])  1.92 us
    pallas_call x1, Pallas kernels, body(): pl.pallas_call(peak_kernel, out_shape=(pltpu.VMEM((n_along, 128), jnp.flo...  1.82 us
    pallas_call x1, Pallas kernels, body(): pl.pallas_call(increment_kernel, out_shape=jax.ShapeDtypeStruct(velocity....  1.45 us
  transfers between devices with their start and end apart: 3, of which 1 were waited for; matrix products, arithmetic and copies ran while one was open for 0% of the time, Pallas kernels for 1%

profile of v9, /device:TPU:1, one launch (start us, length us, event | category | flops | bytes accessed | tf_op | source)
XLA Modules:
  0.0 45.6 jit_solution(7597505447976192606)
XLA Ops:
  0.0 1.8 %peak.1 = (f32[32,128]{1,0:T(8,128)}, f32[3,16,16,256]{3,2,1,0:T(8,128)S(1)}) custom-call(f32[3,16,16,256]{3,2,1,0:T(8,128)} %vel.1), custom_call_target="tpu_custom_call" | custom-call | flops 300000000 | bytes 900000 | tf_op jit(solution)/shard_map/peak/pallas_call | solution.py:167
  1.8 20.6 %all-to-all-start = ((f32[32,1,128]{2,1,0:T(1,128)}), f32[32,1,128]{2,1,0:T(1,128)S(1)}, u32[]{:S(2)}, u32[]{:S(2)}) async-start(f32[32,1,128]{2,1,0:T(1,128)} %bitcast.1), calls=%async_computation | async-start | bytes 32768 | tf_op jit(solution)/shard_map/all_to_all | solution.py:143
  22.4 0.3 edges.1
  22.7 3.4 %collective-permute-start = (f32[9,16,256]{2,1,0:T(8,128)S(1)}, f32[9,16,256]{2,1,0:T(8,128)S(1)}, u32[]{:S(2)}, u32[]{:S(2)}) collective-permute-start(f32[9,16,256]{2,1,0:T(8,128)S(1)} %get-tuple-element.10), channel_id=1, source_target_pairs={{0,8},{8,16},{16,24},{24,32},{32,40},{40,48},{48,56},{56,64},{64,7... | collective-permute-start | bytes 442376 | tf_op jit(solution)/shard_map/ppermute | solution.py:188
  26.1 1.9 %collective-permute-start.1 = (f32[9,16,256]{2,1,0:T(8,128)S(1)}, f32[9,16,256]{2,1,0:T(8,128)S(1)}, u32[]{:S(2)}, u32[]{:S(2)}) collective-permute-start(f32[9,16,256]{2,1,0:T(8,128)S(1)} %get-tuple-element.11), channel_id=1, source_target_pairs={{0,1016},{8,0},{16,8},{24,16},{32,24},{40,32},{48,40},{56,48},{64,... | collective-permute-start | bytes 442376 | tf_op jit(solution)/shard_map/ppermute | solution.py:189
  28.0 3.9 %all-to-all-done = f32[32,1,128]{2,1,0:T(1,128)S(1)} async-done(((f32[32,1,128]{2,1,0:T(1,128)}), f32[32,1,128]{2,1,0:T(1,128)S(1)}, u32[]{:S(2)}, u32[]{:S(2)}) %all-to-all-start) | async-done | bytes 16416 | tf_op jit(solution)/shard_map/all_to_all | solution.py:143
  31.9 12.2 %all_to_all.22 = f32[32,1,128]{2,1,0:T(1,128)S(1)} all-to-all(f32[32,1,128]{2,1,0:T(1,128)S(1)} %bitcast.10), channel_id=1, replica_groups={{516,772,517,515,260,773,771,518,514,261,259,4,774,770,519,513,262,258,..., dimensions={0} | all-to-all | bytes 32768 | tf_op jit(solution)/shard_map/all_to_all | solution.py:143
  44.1 0.0 collective-permute-done.from_left
  44.1 0.0 collective-permute-done.1.from_right
  44.1 1.5 %increment.1 = f32[3,16,16,256]{3,2,1,0:T(8,128)} custom-call(f32[3,16,16,256]{3,2,1,0:T(8,128)S(1)} %get-tuple-element.9.vel, f32[9,16,256]{2,1,0:T(8,128)S(1)} %collective-permute-done.from_left, f32[9,16,256]{2,1,0:T(8,128)S(1)} %collective-permute-done.1.from_right, f32[32,128]{1,0:T(8,128)S(1)} %bitcast.8), custom_call_target="tpu_custom_call" | custom-call | tf_op jit(solution)/shard_map/increment/pallas_call | solution.py:200
  (1 shorter events, 0.0 us)
Async XLA Ops:
  1.8 30.0 %all-to-all-start = ((f32[32,1,128]{2,1,0:T(1,128)}), f32[32,1,128]{2,1,0:T(1,128)S(1)}, u32[]{:S(2)}, u32[]{:S(2)}) async-start(f32[32,1,128]{2,1,0:T(1,128)} %bitcast.1), calls=%async_computation | async-start | bytes 32768 | tf_op jit(solution)/shard_map/all_to_all | solution.py:143
  22.7 21.4 %collective-permute-start = (f32[9,16,256]{2,1,0:T(8,128)S(1)}, f32[9,16,256]{2,1,0:T(8,128)S(1)}, u32[]{:S(2)}, u32[]{:S(2)}) collective-permute-start(f32[9,16,256]{2,1,0:T(8,128)S(1)} %get-tuple-element.10), channel_id=1, source_target_pairs={{0,8},{8,16},{16,24},{24,32},{32,40},{40,48},{48,56},{56,64},{64,7... | collective-permute-start | bytes 442376 | tf_op jit(solution)/shard_map/ppermute | solution.py:188
  26.1 18.0 %collective-permute-start.1 = (f32[9,16,256]{2,1,0:T(8,128)S(1)}, f32[9,16,256]{2,1,0:T(8,128)S(1)}, u32[]{:S(2)}, u32[]{:S(2)}) collective-permute-start(f32[9,16,256]{2,1,0:T(8,128)S(1)} %get-tuple-element.11), channel_id=1, source_target_pairs={{0,1016},{8,0},{16,8},{24,16},{32,24},{40,32},{48,40},{56,48},{64,... | collective-permute-start | bytes 442376 | tf_op jit(solution)/shard_map/ppermute | solution.py:189
